TPU v7x, 128 devices: a whole 4x4x4 slice. The times are simulated.
128 devices in a mesh: rep: 8 (over x_lo, z), shard: 16 (over y, x_hi, core).
Axes of the slice: x: 4 (x_hi: 2, x_lo: 2; x = x_hi * 2 + x_lo), y: 4, z: 4, core: 2. Of those that a mesh axis runs over, the one named last changes fastest.
Arguments:
- tokens: bfloat16 [32768, 8192], P(('rep', 'shard')), may hold values from -6 to 6
- grad_values: bfloat16 [32768, 1024], P(('rep', 'shard')), may hold values from -6 to 6
- weights: bfloat16 [8, 4, 8192, 1024], P('rep', None, 'shard'), may hold values from -0.06629126 to 0.06629126
- fragment: int32 [4], replicated, may hold values from 0 to 3, each once
- anchor: float32 [8192, 1024], P('shard'), may hold values from -0.044194174 to 0.044194174
- momentum: float32 [8192, 1024], P('shard', 'rep'), may hold values from -0.078125 to 0.078125
Outputs:
- values: bfloat16 [32768, 1024], P(('rep', 'shard'))
- grad_tokens: bfloat16 [32768, 8192], P(('rep', 'shard'))
- grad_weight: bfloat16 [8, 8192, 1024], P('rep', 'shard')
- blended: bfloat16 [8, 8192, 1024], P('rep', 'shard')
- new_anchor: float32 [8192, 1024], P('shard')
- new_momentum: float32 [8192, 1024], P('shard', 'rep')
All inputs are finite; a program needn't handle non-finite values.
Results may differ from a plain program's by a relative error of at most 0.00105.
Values may be sent and summed in bfloat16 or wider, within the bound.
No kernel may reach another device: no remote copies, remote signals or barrier semaphores. Data moves between devices by JAX's collectives and lax.ppermute only.
A program may use at most 192 MiB of HBM per device.

v0:
```python
import jax
import jax.numpy as jnp
from jax import lax
from jax.sharding import PartitionSpec as P

outer_momentum = 0.9
outer_rate = 0.7
mix_weight = 0.5


def local(tokens, grad_values, weights, fragment, anchor, momentum):
    chosen = fragment[0]
    worked = fragment[1]
    layers = weights[0]
    synced = lax.dynamic_index_in_dim(layers, chosen, 0, keepdims=False)
    computed = lax.dynamic_index_in_dim(layers, worked, 0, keepdims=False)
    slab_rows = lax.all_gather(computed, "shard", axis=0, tiled=True)
    values_sum = jnp.dot(tokens, slab_rows, preferred_element_type=jnp.float32)
    grad_block = lax.dot_general(
        grad_values, slab_rows, (((1,), (1,)), ((), ())), preferred_element_type=jnp.float32
    )
    token_grad = grad_block
    values_sum, token_grad = (values_sum, token_grad)
    every_grad = lax.all_gather(grad_values, "shard", axis=0, tiled=True)
    own_columns = lax.all_to_all(tokens, "shard", split_axis=1, concat_axis=0, tiled=True)
    weight_sum = lax.dot_general(
        own_columns, every_grad, (((0,), (0,)), ((), ())), preferred_element_type=jnp.float32
    )
    synced_wide = synced.astype(jnp.float32)
    rep_count = lax.axis_size("rep")
    rep_index = lax.axis_index("rep")
    share_cols = momentum.shape[1]
    total = lax.psum(synced_wide, "rep")
    outer_grad = anchor - total / rep_count
    grad_share = lax.dynamic_slice_in_dim(outer_grad, rep_index * share_cols, share_cols, 1)
    new_momentum = outer_momentum * momentum + grad_share
    momentum_full = lax.all_gather(new_momentum, "rep", axis=1, tiled=True)
    new_anchor = anchor - outer_rate * (outer_grad + outer_momentum * momentum_full)
    blended = (mix_weight * synced_wide + (1.0 - mix_weight) * new_anchor).astype(jnp.bfloat16)
    return (
        values_sum.astype(jnp.bfloat16),
        token_grad.astype(jnp.bfloat16),
        weight_sum.astype(jnp.bfloat16)[None],
        blended[None],
        new_anchor,
        new_momentum,
    )


def solution(mesh):
    in_specs = (
        P(("rep", "shard"), None),
        P(("rep", "shard"), None),
        P("rep", None, "shard", None),
        P(),
        P("shard", None),
        P("shard", "rep"),
    )
    out_specs = (
        P(("rep", "shard"), None),
        P(("rep", "shard"), None),
        P("rep", "shard", None),
        P("rep", "shard", None),
        P("shard", None),
        P("shard", "rep"),
    )
    return jax.shard_map(local, mesh=mesh, in_specs=in_specs, out_specs=out_specs, check_vma=False)
```

profile of v0, /device:TPU:1, one launch (start us, length us, event | category | flops | bytes accessed | tf_op | source)
XLA Modules:
  0.0 388.6 jit_solution(16280075750204296466)
XLA Ops:
  7.2 0.0 all-reduce.2.cloned.1.call-start
  7.2 1.3 fusion.18
  12.4 3.5 bitcast_convert_fusion
  15.9 0.0 copy-start
  15.9 0.0 all-reduce.2.cloned.1.call-update
  16.0 0.0 all-gather.7.cloned.1.call-start
  16.0 0.0 copy-start.2
  16.0 82.0 %all-reduce.2.cloned.1.call-done = f32[512,1024]{1,0:T(8,128)} async-done(((f32[512,1024]{1,0:T(8,128)}), f32[512,1024]{1,0:T(8,128)}) %all-reduce.2.cloned.1.call-update) | async-done | bytes 2097168 | tf_op jit(solution)/shard_map/psum | solution.py:33
  98.1 0.0 copy-done
  98.1 2.0 multiply_subtract_fusion.1
  100.1 0.0 copy-done.2
  100.1 0.8 dynamic-slice_add_fusion
  100.8 0.0 all-gather.7.cloned.1.call-update
  100.9 0.0 all-gather.5.cloned.1.call-start
  100.9 0.7 all-gather.5.cloned.1.call-update
  101.6 0.0 all-gather.9.cloned.1.call-start
  101.7 0.5 all-gather.9.cloned.1.call-update
  102.2 6.4 %copy.16 = bf16[256,8192]{0,1:T(8,128)(2,1)} copy(bf16[256,8192]{1,0:T(8,128)(2,1)} %param.6) | data formatting | bytes 8388608 | tf_op args[0]
  108.6 84.0 %all_to_all.19 = bf16[256,16,512]{0,2,1:T(8,128)(2,1)} all-to-all(bf16[256,16,512]{0,2,1:T(8,128)(2,1)} %bitcast.36), channel_id=1, replica_groups=mesh['rep'=8,'shard'=16] {'shard'}, dimensions={1} | all-to-all | bytes 8388608 | tf_op jit(solution)/shard_map/all_to_all | solution.py:25
  192.5 6.4 %copy.17 = bf16[16,256,512]{2,1,0:T(8,128)(2,1)} copy(bf16[16,256,512]{1,2,0:T(8,128)(2,1)} %bitcast.35) | data formatting | bytes 8388608 | tf_op jit(solution)/shard_map/all_to_all | solution.py:25
  198.9 0.0 all-gather.7.cloned.1.call-done
  198.9 5.3 %fusion.17 = (bf16[1,512,1024]{2,1,0:T(8,128)(2,1)}, f32[512,1024]{1,0:T(8,128)}) fusion(bf16[1,4,512,1024]{3,2,1,0:T(8,128)(2,1)} %param.8, s32[]{:T(128)S(6)} %select_n.11, f32[512,1024]{1,0:T(8,128)S(1)} %copy-done, f32[512,1024]{1,0:T(8,128)} %all-gather.7.cloned.1.call-done, f32[512,1024]{1,0:T(8,128)} %all-reduce.2.cloned.1.call-done), kind=kLoop, calls=%fused_computation.13 | loop fusion | flops 5242880 | bytes 10485764 | tf_op jit(solution)/shard_map/broadcast_in_dim | solution.py:44
  204.2 37.4 %all-gather.5.cloned.1.call-done = bf16[4096,1024]{1,0:T(8,128)(2,1)} async-done(((bf16[256,1024]{1,0:T(8,128)(2,1)}), bf16[4096,1024]{1,0:T(8,128)(2,1)}) %all-gather.5.cloned.1.call-update) | async-done | bytes 8388624 | tf_op jit(solution)/shard_map/all_gather | solution.py:24
  241.6 10.1 %fusion.10 = bf16[1,512,1024]{2,1,0:T(8,128)(2,1)} fusion(bf16[4096,512]{1,0:T(8,128)(2,1)} %bitcast.37, bf16[4096,1024]{1,0:T(8,128)(2,1)} %all-gather.5.cloned.1.call-done), kind=kOutput, calls=%fused_computation.10 | convolution fusion | flops 4295491584 | bytes 13631488 | tf_op jit(solution)/shard_map/dot_general | solution.py:26
  251.7 0.0 copy-start.1
  251.7 99.2 %all-gather.9.cloned.1.call-done = bf16[1,1,8192,1024]{3,2,1,0:T(8,128)(2,1)} async-done(((bf16[1,1,512,1024]{3,2,1,0:T(8,128)(2,1)}), bf16[1,1,8192,1024]{3,2,1,0:T(8,128)(2,1)}) %all-gather.9.cloned.1.call-update) | async-done | bytes 16777232 | tf_op jit(solution)/shard_map/all_gather | solution.py:17
  350.9 11.5 %fusion.14 = bf16[256,1024]{0,1:T(8,128)(2,1)S(1)} fusion(bf16[256,8192]{1,0:T(8,128)(2,1)} %param.6, bf16[1,1,8192,1024]{3,2,1,0:T(8,128)(2,1)} %all-gather.9.cloned.1.call-done), kind=kOutput, calls=%fused_computation.12 | convolution fusion | flops 4295229440 | bytes 21495808 | tf_op jit(solution)/shard_map/dot_general | solution.py:18
  362.4 1.0 copy.18
  363.4 0.0 copy-done.1
  363.4 12.3 %fusion.7 = bf16[256,8192]{0,1:T(8,128)(2,1)} fusion(bf16[256,1024]{1,0:T(8,128)(2,1)S(1)} %copy-done.1, bf16[1,1,8192,1024]{3,2,1,0:T(8,128)(2,1)} %all-gather.9.cloned.1.call-done), kind=kOutput, calls=%fused_computation.5 | convolution fusion | flops 4297064448 | bytes 21495808 | tf_op jit(solution)/shard_map/dot_general | solution.py:19
  375.7 6.3 %copy.19 = bf16[256,8192]{1,0:T(8,128)(2,1)} copy(bf16[256,8192]{0,1:T(8,128)(2,1)} %fusion.7) | data formatting | bytes 8388608
Async XLA Ops:
  7.2 90.9 %all-reduce.2.cloned.1.call-start = ((), (), s32[]{:S(2)}) async-start(), calls=%async_computation.2 | async-start | bytes 4194304 | tf_op jit(solution)/shard_map/psum | solution.py:33
  15.9 82.1 %copy-start = (f32[512,1024]{1,0:T(8,128)S(1)}, f32[512,1024]{1,0:T(8,128)}, u32[]{:S(2)}) copy-start(f32[512,1024]{1,0:T(8,128)} %param.10) | copy-start | bytes 6291460
  16.0 183.0 %all-gather.7.cloned.1.call-start = ((), (), s32[]{:S(2)}) async-start(), calls=%async_computation.3 | async-start | bytes 2359296 | tf_op jit(solution)/shard_map/all_gather | solution.py:37
  16.0 84.1 %copy-start.2 = (f32[512,128]{1,0:T(8,128)S(1)}, f32[512,128]{1,0:T(8,128)}, u32[]{:S(2)}) copy-start(f32[512,128]{1,0:T(8,128)} %param.11) | copy-start | bytes 786436
  100.9 140.7 %all-gather.5.cloned.1.call-start = ((), (), s32[]{:S(2)}) async-start(), calls=%async_computation.1 | async-start | bytes 8912896 | tf_op jit(solution)/shard_map/all_gather | solution.py:24
  101.6 249.3 %all-gather.9.cloned.1.call-start = ((), (), s32[]{:S(2)}) async-start(), calls=%async_computation.4 | async-start | bytes 17825792 | tf_op jit(solution)/shard_map/all_gather | solution.py:17
  251.7 111.7 %copy-start.1 = (bf16[256,1024]{1,0:T(8,128)(2,1)S(1)}, bf16[256,1024]{1,0:T(8,128)(2,1)}, u32[]{:S(2)}) copy-start(bf16[256,1024]{1,0:T(8,128)(2,1)} %param.7) | copy-start | bytes 1572868
Sparse Core Ops, SparseCore 0:
  16.1 81.9 all-reduce.1
  101.0 57.1 all-gather.6
  160.7 80.8 all-gather.4
  243.9 106.9 all-gather.8
where the time goes:
time: 389 us
  waiting for transfers between devices  220 us (57%)
  blocking collectives  84 us (22%)
  matrix products  33.9 us (9%)
  local copies, waits for them, and re-layouts  21.4 us (6%)
  between operations  17.7 us (5%)
  other arithmetic  11.6 us (3%)
    all_gather x1, waiting for transfers between devices, local(): slab_rows = lax.all_gather(computed, 'shard', axis=0, tiled=True)  99.2 us
    all_to_all x1, blocking collectives, local(): lax.all_to_all(tokens, 'shard', split_axis=1, concat_axis=0, tiled=True)  84 us
    psum x1, waiting for transfers between devices, local(): total = lax.psum(synced_wide, 'rep')  82 us
    all_gather x1, waiting for transfers between devices, local(): every_grad = lax.all_gather(grad_values, 'shard', axis=0, tiled=True)  37.4 us
    unnamed x9, local copies, waits for them, and re-layouts  13.7 us
    dot_general x1, matrix products, local(): lax.dot_general(grad_values, slab_rows, (((1,), (1,)), ((), ())), preferr...  12.3 us
    dot_general x1, matrix products, local(): values_sum = jnp.dot(tokens, slab_rows, preferred_element_type=jnp.float32)  11.5 us
    dot_general x1, matrix products, local(): lax.dot_general(own_columns, every_grad, (((0,), (0,)), ((), ())), prefer...  10.1 us
  transfers between devices with their start and end apart: 4, of which 3 were waited for; matrix products, arithmetic and copies ran while one was open for 7% of the time, Pallas kernels for 0%

commit v1 on v0

v1 whole, which is shorter than its diff:
```python
import jax
import jax.numpy as jnp
from jax import lax
from jax.experimental import pallas as pl
from jax.experimental.pallas import tpu as pltpu
from jax.sharding import PartitionSpec as P

outer_momentum = 0.9
outer_rate = 0.7
mix_weight = 0.5

NY = 4
VMEM = 60 * 2**20
BLOCK = 512
HALF = 256
SIDES = [(dx, dy) for dx in (1, 0) for dy in range(NY)]

X_SWAP = [(s, s ^ 2) for s in range(16)]
CORE_SWAP = [(s, s ^ 1) for s in range(16)]
LINES = [[y * 4 + k for y in range(NY)] for k in range(4)]
CHIP_LINES = [[y * 4 + xh * 2 + c for y in range(NY) for c in range(2)] for xh in range(2)]


def y_shift(d):
    return [(s, ((s // 4 + d) % NY) * 4 + s % 4) for s in range(16)]


def send(x, pairs):
    return lax.ppermute(x, "shard", pairs)


def z_shift(d):
    return [(r, (r // 4) * 4 + (r + d) % 4) for r in range(8)]


def rep_swap(x, bit):
    return lax.ppermute(x, "rep", [(r, r ^ bit) for r in range(8)])


def line_gather(x, groups):
    return lax.all_gather(x, "shard", axis=0, tiled=True, axis_index_groups=groups)


def wide_dot(a, b, dims):
    return lax.dot_general(a, b, (dims, ((), ())), preferred_element_type=jnp.float32)


class Spot:
    def __init__(self):
        me = lax.axis_index("shard")
        self.y, self.xh, self.core = me // 4, (me // 2) % 2, me % 2
        self.x_lo, self.z = lax.axis_index("rep") // 4, lax.axis_index("rep") % 4

    def row(self, dy):
        return (self.y + dy) % NY

    def columns(self, y, dx, cls, part=0, width=BLOCK):
        block = y * 4 + (self.xh ^ dx) * 2 + (self.core ^ cls)
        return pl.ds(pl.multiple_of(block * BLOCK + part, HALF), width)

    def tokens(self, cls):
        return pl.ds(pl.multiple_of((self.core ^ cls) * HALF, HALF), HALF)


def at(start, size):
    return pl.ds(pl.multiple_of(start, HALF), size)


def move(name, srcs, outs, plan, pick=None, keep=(), deps=()):
    srcs, outs, keep, deps = list(srcs), list(outs), list(keep), list(deps)
    n_pick = 0 if pick is None else 1
    n_in = n_pick + len(srcs) + len(keep) + len(deps)
    n_out = len(outs) + len(keep)
    shapes, n_stores = [], 0
    if plan is not None:

        class Origin:
            y = xh = core = x_lo = z = 0
            row = lambda self, dy: dy
            columns = lambda self, *a: None
            tokens = lambda self, c: None

        draft = plan(Origin(), [0] * 4)
        shapes = [(job[2], srcs[job[0]].dtype) for job in draft]
        n_stores = sum(len(job[3]) for job in draft)

    def body(*refs):
        if plan is None:
            return
        src_refs = refs[n_pick : n_pick + len(srcs)]
        out_refs = refs[n_in : n_in + n_out]
        held, (sems_in, sems_out) = refs[n_in + n_out : -2], refs[-2:]
        jobs = plan(Spot(), refs[0] if n_pick else None)
        loads, stores = [], []
        for n, (i, index, _, _) in enumerate(jobs):
            cp = pltpu.make_async_copy(src_refs[i].at[index], held[n], sems_in.at[n])
            cp.start()
            loads.append(cp)
        for n, (_, _, _, writes) in enumerate(jobs):
            loads[n].wait()
            for j, index, part in writes:
                src = held[n] if part is None else held[n].at[part]
                cp = pltpu.make_async_copy(src, out_refs[j].at[index], sems_out.at[len(stores)])
                cp.start()
                stores.append(cp)
        for cp in stores:
            cp.wait()

    anywhere = pl.BlockSpec(memory_space=pl.ANY)
    scratch = [pltpu.VMEM(shape, dtype) for shape, dtype in shapes]
    if shapes:
        scratch += [pltpu.SemaphoreType.DMA((len(shapes),)), pltpu.SemaphoreType.DMA((n_stores,))]
    args = ([] if pick is None else [pick]) + srcs + keep + deps
    return list(
        pl.pallas_call(
            body,
            out_shape=[jax.ShapeDtypeStruct(o.shape, o.dtype) for o in outs + keep],
            in_specs=[pl.BlockSpec(memory_space=pltpu.SMEM)] * n_pick + [anywhere] * (n_in - n_pick),
            out_specs=[anywhere] * n_out,
            scratch_shapes=scratch,
            input_output_aliases={n_pick + len(srcs) + k: len(outs) + k for k in range(len(keep))},
            compiler_params=pltpu.CompilerParams(vmem_limit_bytes=VMEM),
            cost_estimate=pl.CostEstimate(flops=1, bytes_accessed=1, transcendentals=0),
            name=name,
        )(*args)
    )


def bf16(*shape):
    return jax.ShapeDtypeStruct(shape, jnp.bfloat16)


def place_columns(parts, width, into=None):
    rows = parts[0][0].shape[0]
    srcs = [p[0] for p in parts]
    last = 0

    def plan(spot, _):
        jobs = []
        for i, (_, cls, pieces) in enumerate(parts):
            for k, (y, dx, h) in enumerate(pieces):
                cut = (pl.ds(0, rows), pl.ds(k * HALF, HALF))
                put = (pl.ds(0, rows), spot.columns(y, dx, cls, h * HALF, HALF))
                jobs.append((i, cut, (rows, HALF), [(last, put, None)]))
        return jobs

    outs, keep = ([bf16(rows, width)], []) if into is None else ([], [into])
    return move("place_columns", srcs, outs, plan, keep=keep)[0]


def split_half(total, here):
    width = total.shape[1] // 2
    cut = lambda k: lax.dynamic_slice_in_dim(total, k * width, width, 1)
    return cut(here), cut(1 - here)


def local(tokens, grad_values, weights, fragment, anchor, momentum):
    me, rep = lax.axis_index("shard"), lax.axis_index("rep")
    y, core = me // 4, me % 2
    x_lo, z_hi, z_lo = rep // 4, (rep // 2) % 2, rep % 2
    cols = grad_values.shape[1]
    rows = tokens.shape[0]
    top, low = pl.ds(0, HALF), pl.ds(HALF, HALF)
    every, half = pl.ds(0, BLOCK), (HALF, cols)

    wb, wa = move(
        "pick_rows",
        [weights],
        [bf16(*half), bf16(*half)],
        lambda spot, f: [(0, (0, f[1], low), half, [(0, (top,), None)]), (0, (0, f[1], top), half, [(1, (top,), None)])],
        pick=fragment,
    )
    wb_line = line_gather(wb, LINES)
    wa_x = send(wa, X_SWAP)

    def split(spot, f):
        jobs = [
            (0, (top, spot.columns(spot.row(dy), dx, 1)), (rows, BLOCK), [(0, (n,), None)])
            for n, (dx, dy) in enumerate(SIDES)
        ]
        jobs.append((1, (top,), half, [(1, (top,), None)]))
        side = (1 - spot.x_lo) * (cols // 2)
        jobs.append((2, (0, f[0], every, at(side, cols // 2)), (BLOCK, cols // 2), [(2, (every,), None)]))
        for n, (dx, dy) in enumerate(SIDES):
            writes = [(3 + n, (spot.tokens(0),), None)] + spread(spot, dx, dy, top, 11)
            jobs.append((0, (top, spot.columns(spot.row(dy), dx, 0)), (rows, BLOCK), writes))
        return jobs

    def spread(spot, dx, dy, where, first):
        yy = spot.row(dy)
        return [
            (first + dx, (where, at(yy * HALF, HALF)), (top, low)),
            (first + 2, (where, at(yy * BLOCK + dx * HALF, HALF)), (top, top)),
        ]

    x_other, g_own, away, *x_parts = move(
        "split_tokens",
        [tokens, grad_values, weights],
        [bf16(8, rows, BLOCK), bf16(*half), bf16(BLOCK, cols // 2)]
        + [bf16(BLOCK, BLOCK)] * 8
        + [bf16(BLOCK, NY * HALF)] * 2
        + [bf16(BLOCK, NY * BLOCK)],
        split,
        pick=fragment,
        deps=[wb],
    )
    x_other = send(x_other, CORE_SWAP)
    g_line = line_gather(g_own, CHIP_LINES)
    came = rep_swap(away, 4)

    def fill(spot, _):
        return [
            (0, (n,), (rows, BLOCK), [(n, (spot.tokens(1),), None)] + spread(spot, dx, dy, low, 8))
            for n, (dx, dy) in enumerate(SIDES)
        ]

    x_parts = move("fill_tokens", [x_other], [], fill, keep=x_parts)
    s1, s0, x_b, x_a = x_parts[:4], x_parts[4:8], x_parts[8:10], x_parts[10]

    l1, r1, o1 = send(s1[1], y_shift(1)), send(s1[3], y_shift(-1)), send(s1[2], y_shift(2))

    wa_pair, wb_line, came = move(
        "a_pair",
        [wa, wa_x],
        [bf16(BLOCK, cols)],
        lambda *_: [(0, (top,), half, [(0, (top,), None)]), (1, (top,), half, [(0, (low,), None)])],
        keep=[wb_line, came],
        deps=[l1, r1],
    )
    wb_line_x = send(wb_line, X_SWAP)
    wa_line = line_gather(wa_pair, LINES)

    synced = lax.dynamic_index_in_dim(weights[0], fragment[0], 0, keepdims=False)
    share_cols = momentum.shape[1]

    mine = lax.dynamic_slice_in_dim(synced, x_lo * (cols // 2), cols // 2, 1).astype(jnp.float32)
    total = mine + came.astype(jnp.float32)
    total, away = split_half(total, z_hi)
    came = rep_swap(away, 2)

    line = tuple(enumerate((0, -1, 1, 2)))
    line1_top, line1_low, s0[1], s0[3], came = move(
        "line_across",
        [s1[0], l1, r1, o1],
        [bf16(NY * BLOCK, HALF)] * 2,
        lambda spot, _: [
            (
                n,
                (every,),
                (BLOCK, BLOCK),
                [(h, (at(spot.row(dy) * BLOCK, BLOCK),), (every, cut)) for h, cut in enumerate((top, low))],
            )
            for n, dy in line
        ],
        keep=[s0[1], s0[3], came],
    )
    l0, r0 = send(s0[1], y_shift(1)), send(s0[3], y_shift(-1))
    total, away = split_half(total + came, z_lo)
    total = total + rep_swap(away, 1)
    anchor_share = lax.dynamic_slice_in_dim(anchor, rep * share_cols, share_cols, 1)
    outer_share = anchor_share - total / lax.axis_size("rep")
    new_momentum = outer_momentum * momentum + outer_share
    found = anchor_share - outer_rate * (outer_share + outer_momentum * new_momentum)
    came = rep_swap(found, 4)

    part1_top = wide_dot(line1_top, g_line, ((0,), (0,)))
    part1_top_x = send(part1_top, X_SWAP)
    part1_low = wide_dot(line1_low, g_line, ((0,), (0,)))

    f32 = lambda count: jax.ShapeDtypeStruct((BLOCK, count * share_cols), jnp.float32)
    blocks = lambda k, count=1: (every, pl.ds(pl.multiple_of(k * share_cols, share_cols), count * share_cols))

    def beside(count, here):
        def plan(spot, _):
            mine = here(spot)
            return [
                (i, (every,), (BLOCK, count * share_cols), [(0, blocks(k * count, count), None)])
                for i, k in enumerate((mine, 1 - mine))
            ]

        return plan

    x_b = move("after_part", [], [], None, keep=x_b, deps=[part1_top, part1_low])

    (s0[2],) = move("last_cols", [], [], None, keep=[s0[2]], deps=[l0, r0, part1_top, part1_low])
    o0 = send(s0[2], y_shift(2))
    g_beside = lax.dynamic_slice_in_dim(g_line, y * BLOCK + (1 - core) * HALF, HALF, 0)
    g_pair = jnp.concatenate([grad_values, g_beside], 0)

    def both(x_part, w_rows, pieces):
        v = wide_dot(x_part, w_rows, ((1,), (0,)))
        gx = wide_dot(g_pair, w_rows, ((1,), (1,))).astype(jnp.bfloat16)
        return v, [(gx[:HALF], 0, pieces), (send(gx[HALF:], CORE_SWAP), 1, pieces)]

    v_b0, gx_b0 = both(x_b[0], wb_line, [(yy, 0, 1) for yy in range(NY)])

    v_b1, gx_b1 = both(x_b[1], wb_line_x, [(yy, 1, 1) for yy in range(NY)])
    v_b = v_b0 + v_b1

    found, part1_low = move(
        "last_part",
        [found, came],
        [f32(2)],
        beside(1, lambda spot: spot.x_lo),
        keep=[part1_low],
        deps=[part1_top_x, o0, v_b, gx_b0[0][0], gx_b1[0][0]],
    )
    part1_low_x = send(part1_low, X_SWAP)
    shares = [found] + [lax.ppermute(found, "rep", z_shift(d)) for d in (1, -1, 2)]

    v_a, gx_a = both(x_a, wa_line, [(yy, dx, 0) for yy in range(NY) for dx in range(2)])
    v = v_b + v_a

    def anchor_columns(spot, _):
        return [
            (i, blocks(xx), (BLOCK, share_cols), [(0, blocks(xx * 4 + (spot.z + dz) % 4), None)])
            for i, dz in enumerate((0, 3, 1, 2))
            for xx in range(2)
        ]

    (new_anchor,) = move("anchor_columns", shares, [f32(8)], anchor_columns)
    blended = (mix_weight * synced.astype(jnp.float32) + (1.0 - mix_weight) * new_anchor).astype(jnp.bfloat16)

    values = (v[:HALF] + send(v[HALF:], CORE_SWAP)).astype(jnp.bfloat16)
    token_grad = place_columns(gx_b0 + gx_b1, tokens.shape[1])
    token_grad = place_columns(gx_a, tokens.shape[1], token_grad)

    (line0,) = move(
        "line_own",
        [s0[0], l0, r0, o0],
        [bf16(NY * BLOCK, BLOCK)],
        lambda spot, _: [
            (n, (every,), (BLOCK, BLOCK), [(0, (at(spot.row(dy) * BLOCK, BLOCK),), None)]) for n, dy in line
        ],
        deps=[part1_low],
    )
    part0 = wide_dot(line0, g_line, ((0,), (0,)))
    (part1_low_x,) = move("rest", [], [], None, keep=[part1_low_x], deps=[part0, new_anchor])
    grad_weight = (part0 + jnp.concatenate([part1_top_x, part1_low_x], 0)).astype(jnp.bfloat16)

    return values, token_grad, grad_weight[None], blended[None], new_anchor, new_momentum


def solution(mesh):
    in_specs = (
        P(("rep", "shard"), None),
        P(("rep", "shard"), None),
        P("rep", None, "shard", None),
        P(),
        P("shard", None),
        P("shard", "rep"),
    )
    out_specs = (
        P(("rep", "shard"), None),
        P(("rep", "shard"), None),
        P("rep", "shard", None),
        P("rep", "shard", None),
        P("shard", None),
        P("shard", "rep"),
    )
    return jax.shard_map(local, mesh=mesh, in_specs=in_specs, out_specs=out_specs, check_vma=False)
```

time: 389 us -> 197 us (0.51)
  waiting for transfers between devices: 220 us -> 60.1 us
  blocking collectives: 84 us -> 0 us
  starting transfers between devices: 0.16 us -> 38 us
  Pallas kernels: 0 us -> 28.5 us
  matrix products: 33.9 us -> 27.2 us
  local copies, waits for them, and re-layouts: 21.4 us -> 15.4 us
    all_gather x3, waiting for transfers between devices: 137 us -> 16.9 us  [line_gather(): lax.all_gather(x, 'shard', axis=0, tiled=True, axis_index_groups=groups)]
    all_to_all x1 -> x0, blocking collectives: 84 us -> none  [local(): lax.all_to_all(tokens, 'shard', split_axis=1, concat_axis=0, tiled=True)]
    psum x1 -> x0, waiting for transfers between devices: 82 us -> none  [local(): total = lax.psum(synced_wide, 'rep')]
    ppermute x0 -> x22, waiting for transfers between devices: none -> 43.2 us  [the longest x15 36.1 us: send(): return lax.ppermute(x, 'shard', pairs)]
    ppermute x0 -> x22, starting transfers between devices: none -> 37.9 us  [the longest x15 29 us: send(): return lax.ppermute(x, 'shard', pairs)]
    pallas_call x0 -> x13, Pallas kernels: none -> 28.5 us  [move(): pl.pallas_call(body, out_shape=[jax.ShapeDtypeStruct(o.shape, o.dtype) fo...]
    dot_general x3 -> x9, matrix products: 33.9 us -> 27.2 us  [wide_dot(): lax.dot_general(a, b, (dims, ((), ())), preferred_element_type=jnp.float32)]
    all_to_all x1 -> x0, local copies, waits for them, and re-layouts: 6.41 us -> none  [local(): lax.all_to_all(tokens, 'shard', split_axis=1, concat_axis=0, tiled=True)]
  transfers between devices with their start and end apart: 4 -> 25, of which waited for: 3 -> 12; matrix products, arithmetic and copies ran while one was open for 7% -> 23% of each run, Pallas kernels for 0% -> 12%
where the time goes in v1:
time: 197 us; the launch traced here: 196 us
  waiting for transfers between devices  60.1 us (31%)
  starting transfers between devices  38 us (19%)
  Pallas kernels  28.5 us (14%)
  matrix products  27.2 us (14%)
  local copies, waits for them, and re-layouts  15.4 us (8%)
  between operations  14.3 us (7%)
  other arithmetic  12.5 us (6%)
    ppermute x15, waiting for transfers between devices, send(): return lax.ppermute(x, 'shard', pairs)  36.1 us
    ppermute x15, starting transfers between devices, send(): return lax.ppermute(x, 'shard', pairs)  29 us
    pallas_call x13, Pallas kernels, move(): pl.pallas_call(body, out_shape=[jax.ShapeDtypeStruct(o.shape, o.dtype) fo...  28.5 us
    dot_general x9, matrix products, wide_dot(): lax.dot_general(a, b, (dims, ((), ())), preferred_element_type=jnp.float32)  27.2 us
    all_gather x3, waiting for transfers between devices, line_gather(): lax.all_gather(x, 'shard', axis=0, tiled=True, axis_index_groups=groups)  16.9 us
    unnamed x76, local copies, waits for them, and re-layouts  9.31 us
    ppermute x4, waiting for transfers between devices, rep_swap(): return lax.ppermute(x, 'rep', [(r, r ^ bit) for r in range(8)])  7.1 us
    ppermute x4, starting transfers between devices, rep_swap(): return lax.ppermute(x, 'rep', [(r, r ^ bit) for r in range(8)])  5.99 us
  transfers between devices with their start and end apart: 25, of which 12 were waited for; matrix products, arithmetic and copies ran while one was open for 23% of the time, Pallas kernels for 12%

profile of v1, /device:TPU:1, one launch (start us, length us, event | category | flops | bytes accessed | tf_op | source)
XLA Modules:
  0.0 196.0 jit_solution(15645583111560557879)
XLA Ops:
  7.2 2.7 %pick_rows.1 = (bf16[256,1024]{1,0:T(8,128)(2,1)}, bf16[256,1024]{1,0:T(8,128)(2,1)}) custom-call(s32[4]{0:T(128)} %refs_0_.3, bf16[1,4,512,1024]{3,2,1,0:T(8,128)(2,1)} %refs_3_.1), custom_call_target="tpu_custom_call" | custom-call | flops 1 | bytes 1 | tf_op jit(solution)/shard_map/pick_rows/pallas_call | solution.py:115
  10.0 6.2 %split_tokens.1 = (bf16[8,256,512]{2,1,0:T(8,128)(2,1)}, bf16[256,1024]{1,0:T(8,128)(2,1)}, bf16[512,512]{1,0:T(8,128)(2,1)}, bf16[512,512]{1,0:T(8,128)(2,1)}, ...) custom-call(s32[4]{0:T(128)} %refs_0_.3, ...), custom_call_target="tpu_custom_call" | custom-call | flops 1 | bytes 1 | tf_op jit(solution)/shard_map/split_tokens/pallas_call | solution.py:115
  16.3 1.5 collective-permute-start
  17.8 1.3 collective-permute-start.5
  19.1 2.5 %collective-permute-start.4 = (bf16[256,1024]{1,0:T(8,128)(2,1)S(1)}, bf16[256,1024]{1,0:T(8,128)(2,1)S(1)}, u32[]{:S(2)}, u32[]{:S(2)}) collective-permute-start(bf16[256,1024]{1,0:T(8,128)(2,1)S(1)} %copy-done.22), channel_id=1, source_target_pairs={{0,2},{1,3},{2,0},{3,1},{4,6},{5,7},{6,4},{7,5},{8,10},{9,11},{10,... | collective-permute-start | bytes 1572872 | tf_op jit(solution)/shard_map/ppermute | solution.py:29
  21.8 1.3 copy-done.7
  23.1 3.2 %fill_tokens.1 = (bf16[512,512]{1,0:T(8,128)(2,1)}, bf16[512,512]{1,0:T(8,128)(2,1)}, bf16[512,512]{1,0:T(8,128)(2,1)}, bf16[512,512]{1,0:T(8,128)(2,1)}, bf16[5...) custom-call(bf16[8,256,512]{2,1,0:T(8,128)(2,1)} %copy-done.7, ...), custom_call_target="tpu_custom_call", output_to_operand_aliasing={{0}: (1, {}), {1}: (2, {}), {2}: (3, {}), {3}: (4, {}), {4}... | custom-call | flops 1 | bytes 1 | tf_op jit(solution)/shard_map/fill_tokens/pallas_call | solution.py:115
  26.3 1.4 collective-permute-start.1
  27.8 1.5 collective-permute-start.2
  29.3 2.2 %collective-permute-done.5.refs_3_ = bf16[512,512]{1,0:T(8,128)(2,1)S(1)} collective-permute-done((bf16[512,512]{1,0:T(8,128)(2,1)}, bf16[512,512]{1,0:T(8,128)(2,1)S(1)}, u32[]{:S(2)}, u32[]{:S(2)}) %collective-permute-start.5) | collective-permute-done | bytes 524320 | tf_op jit(solution)/shard_map/ppermute | solution.py:37
  31.6 13.4 %collective-permute-done.4.refs_1_ = bf16[256,1024]{1,0:T(8,128)(2,1)S(1)} collective-permute-done((bf16[256,1024]{1,0:T(8,128)(2,1)S(1)}, bf16[256,1024]{1,0:T(8,128)(2,1)S(1)}, u32[]{:S(2)}, u32[]{:S(2)}) %collective-permute-start.4) | collective-permute-done | bytes 524320 | tf_op jit(solution)/shard_map/ppermute | solution.py:29
  45.0 8.0 %collective-permute-done.1.refs_4_.refs_1_ = bf16[512,512]{1,0:T(8,128)(2,1)S(1)} collective-permute-done((bf16[512,512]{1,0:T(8,128)(2,1)}, bf16[512,512]{1,0:T(8,128)(2,1)S(1)}, u32[]{:S(2)}, u32[]{:S(2)}) %collective-permute-start.1) | collective-permute-done | bytes 524320 | tf_op jit(solution)/shard_map/ppermute | solution.py:29
  53.0 2.5 %all-gather.4.cloned.1.call-done.refs_2_ = bf16[1024,1024]{1,0:T(8,128)(2,1)} async-done(((bf16[256,1024]{1,0:T(8,128)(2,1)}), bf16[1024,1024]{1,0:T(8,128)(2,1)}) %all-gather.4.cloned.1.call-update) | async-done | bytes 2097168 | tf_op jit(solution)/shard_map/all_gather | solution.py:41
  55.5 2.1 %a_pair.1 = (bf16[512,1024]{1,0:T(8,128)(2,1)}, bf16[1024,1024]{1,0:T(8,128)(2,1)}, bf16[512,512]{1,0:T(8,128)(2,1)}) custom-call(bf16[256,1024]{1,0:T(8,128)(2,1)} %get-tuple-element.66.refs_0_, bf16[256,1024]{1,0:T(8,128)(2,1)} %copy-done.23, ...), custom_call_target="tpu_custom_call", output_to_operand_aliasing={{1}: (2, {}), {2}: (3, {})} | custom-call | flops 1 | bytes 1 | tf_op jit(solution)/shard_map/a_pair/pallas_call | solution.py:115
  57.8 1.6 collective-permute-start.3
  59.4 1.5 convert_add_fusion.1
  61.0 2.9 %collective-permute-start.6 = (f32[512,256]{1,0:T(8,128)S(1)}, f32[512,256]{1,0:T(8,128)S(1)}, u32[]{:S(2)}, u32[]{:S(2)}) collective-permute-start(f32[512,256]{1,0:T(8,128)S(1)} %constant_dynamic-slice_fusion.2), channel_id=1, source_target_pairs={{0,32},{16,48},{32,0},{48,16},{64,96},{80,112},{96,64},{112,80},{1... | collective-permute-start | bytes 1572872 | tf_op jit(solution)/shard_map/ppermute | solution.py:37
  63.9 2.7 %collective-permute-start.7 = (bf16[1024,1024]{1,0:T(8,128)(2,1)}, bf16[1024,1024]{1,0:T(8,128)(2,1)}, u32[]{:S(2)}, u32[]{:S(2)}) collective-permute-start(bf16[1024,1024]{1,0:T(8,128)(2,1)} %get-tuple-element.73), channel_id=1, source_target_pairs={{0,2},{1,3},{2,0},{3,1},{4,6},{5,7},{6,4},{7,5},{8,10},{9,11},{10,... | collective-permute-start | bytes 6291464 | tf_op jit(solution)/shard_map/ppermute | solution.py:29
  66.6 6.2 %collective-permute-done.3.refs_3_ = bf16[512,512]{1,0:T(8,128)(2,1)S(1)} collective-permute-done((bf16[512,512]{1,0:T(8,128)(2,1)S(1)}, bf16[512,512]{1,0:T(8,128)(2,1)S(1)}, u32[]{:S(2)}, u32[]{:S(2)}) %collective-permute-start.3) | collective-permute-done | bytes 524320 | tf_op jit(solution)/shard_map/ppermute | solution.py:29
  72.8 2.3 %collective-permute-done.6.refs_6_ = f32[512,256]{1,0:T(8,128)S(1)} collective-permute-done((f32[512,256]{1,0:T(8,128)S(1)}, f32[512,256]{1,0:T(8,128)S(1)}, u32[]{:S(2)}, u32[]{:S(2)}) %collective-permute-start.6) | collective-permute-done | bytes 524320 | tf_op jit(solution)/shard_map/ppermute | solution.py:37
  75.9 2.5 %line_across.1 = (bf16[2048,256]{1,0:T(8,128)(2,1)}, bf16[2048,256]{1,0:T(8,128)(2,1)}, bf16[512,512]{1,0:T(8,128)(2,1)}, bf16[512,512]{1,0:T(8,128)(2,1)}, f32[512,256]{1,0:T(8,128)}) custom-call(bf16[512,512]{1,0:T(8,128)(2,1)} %get-tuple-element.60.refs_0_, ...), custom_call_target="tpu_custom_call", output_to_operand_aliasing={{2}: (4, {}), {3}: (5, {}), {4}: (6, {})} | custom-call | flops 1 | bytes 1 | tf_op jit(solution)/shard_map/line_across/pallas_call | solution.py:115
  78.4 1.2 dynamic-slice_add_fusion
  79.7 0.9 collective-permute-start.15
  81.4 1.9 collective-permute-start.13
  83.3 2.6 %collective-permute-done.15 = f32[512,128]{1,0:T(8,128)S(1)} collective-permute-done((f32[512,128]{1,0:T(8,128)S(1)}, f32[512,128]{1,0:T(8,128)S(1)}, u32[]{:S(2)}, u32[]{:S(2)}) %collective-permute-start.15) | collective-permute-done | bytes 262176 | tf_op jit(solution)/shard_map/ppermute | solution.py:37
  85.9 1.7 multiply_subtract_fusion
  87.6 0.8 collective-permute-start.16
  88.4 8.2 %all-gather.6.cloned.1.call-done = bf16[2048,1024]{1,0:T(8,128)(2,1)} async-done(((bf16[256,1024]{1,0:T(8,128)(2,1)}), bf16[2048,1024]{1,0:T(8,128)(2,1)}) %all-gather.6.cloned.1.call-update) | async-done | bytes 4194320 | tf_op jit(solution)/shard_map/all_gather | solution.py:41
  96.7 3.9 %fusion.12.refs_2_.refs_3_ = f32[256,1024]{1,0:T(8,128)S(1)} fusion(bf16[2048,256]{1,0:T(8,128)(2,1)} %get-tuple-element.69, bf16[2048,1024]{1,0:T(8,128)(2,1)} %all-gather.6.cloned.1.call-done), kind=kOutput, calls=%fused_computation.29 | convolution fusion | flops 1073741824 | bytes 6291456 | tf_op jit(solution)/shard_map/dot_general | solution.py:45
  100.6 2.8 %collective-permute-start.17 = (f32[256,1024]{1,0:T(8,128)S(1)}, f32[256,1024]{1,0:T(8,128)S(1)}, u32[]{:S(2)}, u32[]{:S(2)}) collective-permute-start(f32[256,1024]{1,0:T(8,128)S(1)} %fusion.12.refs_2_.refs_3_), channel_id=1, source_target_pairs={{0,2},{1,3},{2,0},{3,1},{4,6},{5,7},{6,4},{7,5},{8,10},{9,11},{10,... | collective-permute-start | bytes 3145736 | tf_op jit(solution)/shard_map/ppermute | solution.py:29
  103.5 2.3 %fusion.13.refs_3_.refs_4_.refs_2_ = f32[256,1024]{1,0:T(8,128)} fusion(bf16[2048,256]{1,0:T(8,128)(2,1)S(1)} %copy-done.37, bf16[2048,1024]{1,0:T(8,128)(2,1)S(1)} %copy-done.33), kind=kOutput, calls=%fused_computation.30 | convolution fusion | flops 1073741824 | bytes 6291456 | tf_op jit(solution)/shard_map/dot_general | solution.py:45
  106.6 2.0 %collective-permute-start.14 = (bf16[512,512]{1,0:T(8,128)(2,1)}, bf16[512,512]{1,0:T(8,128)(2,1)S(1)}, u32[]{:S(2)}, u32[]{:S(2)}) collective-permute-start(bf16[512,512]{1,0:T(8,128)(2,1)} %last_cols.1), channel_id=1, source_target_pairs={{0,8},{1,9},{2,10},{3,11},{4,12},{5,13},{6,14},{7,15},{8,0},{9,1},... | collective-permute-start | bytes 1572872 | tf_op jit(solution)/shard_map/ppermute | solution.py:29
  108.5 1.1 constant_dynamic-slice_fusion.1
  109.7 1.5 collective-permute-done.7
  111.2 3.1 %convolution_convert_fusion.1 = bf16[512,1024]{1,0:T(8,128)(2,1)S(1)} fusion(bf16[1024,1024]{1,0:T(8,128)(2,1)} %collective-permute-done.7, bf16[256,1024]{1,0:T(8,128)(2,1)S(1)} %constant_dynamic-slice_fusion.1, bf16[256,1024]{1,0:T(8,128)(2,1)S(1)} %copy-done.21), kind=kOutput, calls=%fused_computation.8 | convolution fusion | flops 1076363264 | bytes 4194304 | tf_op jit(solution)/shard_map/dot_general | solution.py:45
  114.3 1.0 fusion.10
  115.3 4.6 %collective-permute-start.11 = (bf16[256,1024]{1,0:T(8,128)(2,1)}, bf16[256,1024]{1,0:T(8,128)(2,1)S(1)}, u32[]{:S(2)}, u32[]{:S(2)}) collective-permute-start(bf16[256,1024]{1,0:T(8,128)(2,1)} %get-tuple-element.88), channel_id=1, source_target_pairs={{0,1},{1,0},{2,3},{3,2},{4,5},{5,4},{6,7},{7,6},{8,9},{9,8},{10,11... | collective-permute-start | bytes 1572872 | tf_op jit(solution)/shard_map/ppermute | solution.py:29
  119.9 1.3 convolution_convert_fusion.2
  121.2 1.0 fusion.11
  122.2 0.9 collective-permute-start.10
  123.1 3.3 %fusion.14 = f32[512,1024]{1,0:T(8,128)S(1)} fusion(bf16[512,1024]{1,0:T(8,128)(2,1)} %get-tuple-element.74, bf16[1024,1024]{1,0:T(8,128)(2,1)} %collective-permute-done.7), kind=kOutput, calls=%fused_computation.31 | convolution fusion | flops 1073741824 | bytes 5242880 | tf_op jit(solution)/shard_map/dot_general | solution.py:45
  126.5 2.6 %convolution_add_fusion.1.refs_5_ = f32[512,1024]{1,0:T(8,128)} fusion(f32[512,1024]{1,0:T(8,128)S(1)} %fusion.14, bf16[512,1024]{1,0:T(8,128)(2,1)S(1)} %copy-done.3, bf16[1024,1024]{1,0:T(8,128)(2,1)S(1)} %copy-done.14), kind=kOutput, calls=%fused_computation.7 | convolution fusion | flops 1074266112 | bytes 7340032 | tf_op jit(solution)/shard_map/dot_general | solution.py:45
  129.8 2.6 %place_columns.2.refs_2_ = bf16[256,8192]{1,0:T(8,128)(2,1)} custom-call(bf16[256,1024]{1,0:T(8,128)(2,1)} %get-tuple-element.91.refs_0_.refs_6_, bf16[256,1024]{1,0:T(8,128)(2,1)} %collective-permute-done.10.refs_1_, bf16[256,1024]{1,0:T(8,128)(2,1)} %get-tuple-element.89.refs_2_.refs_7_, bf16[256,1024]{1,0:T(8,128)(2,1)} %copy-done.26), custom_call_target="tpu_custom_call" | custom-call | flops 1 | bytes 1 | tf_op jit(solution)/shard_map/place_columns/pallas_call | solution.py:115
  132.5 6.7 %collective-permute-done.17.refs_3_ = f32[256,1024]{1,0:T(8,128)S(1)} collective-permute-done((f32[256,1024]{1,0:T(8,128)S(1)}, f32[256,1024]{1,0:T(8,128)S(1)}, u32[]{:S(2)}, u32[]{:S(2)}) %collective-permute-start.17) | collective-permute-done | bytes 1048608 | tf_op jit(solution)/shard_map/ppermute | solution.py:29
  139.2 1.0 copy-done.1
  140.1 1.8 last_part.1
  141.9 1.0 collective-permute-start.19
  142.9 1.7 collective-permute-start.20
  144.8 2.8 %collective-permute-start.18 = (f32[256,1024]{1,0:T(8,128)}, f32[256,1024]{1,0:T(8,128)}, u32[]{:S(2)}, u32[]{:S(2)}) collective-permute-start(f32[256,1024]{1,0:T(8,128)} %get-tuple-element.82.refs_4_), channel_id=1, source_target_pairs={{0,2},{1,3},{2,0},{3,1},{4,6},{5,7},{6,4},{7,5},{8,10},{9,11},{10,... | collective-permute-start | bytes 3145736 | tf_op jit(solution)/shard_map/ppermute | solution.py:29
  147.7 2.5 %line_own.1 = bf16[2048,512]{1,0:T(8,128)(2,1)} custom-call(bf16[512,512]{1,0:T(8,128)(2,1)} %get-tuple-element.77.refs_0_, bf16[512,512]{1,0:T(8,128)(2,1)} %copy-done.19, bf16[512,512]{1,0:T(8,128)(2,1)} %collective-permute-done.13.refs_2_, bf16[512,512]{1,0:T(8,128)(2,1)} %copy-done.10, f32[256,1024]{1,0:T(8,128)} %get-tuple-element.82.refs_4_), custom_call_target="tpu_custom_call" | custom-call | flops 1 | bytes 1 | tf_op jit(solution)/shard_map/line_own/pallas_call | solution.py:115
  150.2 6.1 %all-gather.8.cloned.1.call-done = bf16[2048,1024]{1,0:T(8,128)(2,1)} async-done(((bf16[512,1024]{1,0:T(8,128)(2,1)}), bf16[2048,1024]{1,0:T(8,128)(2,1)}) %all-gather.8.cloned.1.call-update) | async-done | bytes 4194320 | tf_op jit(solution)/shard_map/all_gather | solution.py:41
  156.3 4.7 %convolution_convert_fusion = bf16[512,2048]{1,0:T(8,128)(2,1)S(1)} fusion(bf16[2048,1024]{1,0:T(8,128)(2,1)} %all-gather.8.cloned.1.call-done, bf16[256,1024]{1,0:T(8,128)(2,1)S(1)} %copy-done.28, bf16[256,1024]{1,0:T(8,128)(2,1)S(1)} %copy-done.21), kind=kOutput, calls=%fused_computation | convolution fusion | flops 2150629376 | bytes 7340032 | tf_op jit(solution)/shard_map/dot_general | solution.py:45
  161.0 1.7 fusion.9
  164.0 2.4 %convolution_add_fusion = f32[512,1024]{1,0:T(8,128)S(1)} fusion(f32[512,1024]{1,0:T(8,128)S(1)} %copy-done.5, bf16[512,2048]{1,0:T(8,128)(2,1)S(1)} %copy-done.6, bf16[2048,1024]{1,0:T(8,128)(2,1)S(1)} %copy-done.36), kind=kOutput, calls=%fused_computation.6 | convolution fusion | flops 2148007936 | bytes 10485760 | tf_op jit(solution)/shard_map/dot_general | solution.py:45
  166.4 1.1 slice.37
  167.5 1.5 collective-permute-start.8
  169.3 3.7 %fusion.15.refs_1_ = f32[512,1024]{1,0:T(8,128)} fusion(bf16[2048,512]{1,0:T(8,128)(2,1)S(1)} %copy-done.17, bf16[2048,1024]{1,0:T(8,128)(2,1)S(1)} %copy-done.34), kind=kOutput, calls=%fused_computation.32 | convolution fusion | flops 2147483648 | bytes 8388608 | tf_op jit(solution)/shard_map/dot_general | solution.py:45
  173.8 0.8 copy-done.31
  174.6 2.4 %anchor_columns.1.refs_2_ = f32[512,1024]{1,0:T(8,128)} custom-call(f32[512,256]{1,0:T(8,128)} %get-tuple-element.83.refs_0_, f32[512,256]{1,0:T(8,128)} %copy-done.29, f32[512,256]{1,0:T(8,128)} %copy-done.30, f32[512,256]{1,0:T(8,128)} %copy-done.31), custom_call_target="tpu_custom_call" | custom-call | flops 1 | bytes 1 | tf_op jit(solution)/shard_map/anchor_columns/pallas_call | solution.py:115
  177.0 3.2 %fusion.3 = bf16[1,512,1024]{2,1,0:T(8,128)(2,1)} fusion(f32[512,1024]{1,0:T(8,128)} %anchor_columns.1.refs_2_, bf16[1,4,512,1024]{3,2,1,0:T(8,128)(2,1)} %refs_3_.1, s32[]{:T(128)S(6)} %select_n.54), kind=kLoop, calls=%fused_computation.10 | loop fusion | flops 2097152 | bytes 4194308 | tf_op jit(solution)/shard_map/broadcast_in_dim | solution.py:341
  180.2 1.6 copy-done
  182.0 2.7 %fusion.4 = bf16[1,512,1024]{2,1,0:T(8,128)(2,1)} fusion(f32[512,1024]{1,0:T(8,128)S(1)} %copy-done, f32[256,1024]{1,0:T(8,128)} %rest.1, f32[256,1024]{1,0:T(8,128)S(1)} %copy-done.2), kind=kLoop, calls=%fused_computation.11 | loop fusion | flops 1572864 | bytes 5242880 | tf_op jit(solution)/shard_map/broadcast_in_dim | solution.py:341
  184.7 2.2 %fusion.5 = bf16[256,1024]{1,0:T(8,128)(2,1)} fusion(f32[256,1024]{1,0:T(8,128)} %collective-permute-done.8, f32[512,1024]{1,0:T(8,128)S(1)} %copy-done.16), kind=kLoop, calls=%fused_computation.13 | loop fusion | flops 524288 | bytes 2621440 | tf_op jit(solution)/shard_map/convert_element_type | solution.py:324
  186.9 2.6 %place_columns.3 = bf16[256,8192]{1,0:T(8,128)(2,1)} custom-call(bf16[256,2048]{1,0:T(8,128)(2,1)} %get-tuple-element.87.refs_0_, bf16[256,2048]{1,0:T(8,128)(2,1)} %collective-permute-done.9.refs_1_, bf16[256,8192]{1,0:T(8,128)(2,1)} %place_columns.2.refs_2_), custom_call_target="tpu_custom_call", output_to_operand_aliasing={{}: (2, {})} | custom-call | flops 1 | bytes 1 | tf_op jit(solution)/shard_map/place_columns/pallas_call | solution.py:115
  (100 shorter events, 6.5 us)
Async XLA Ops:
  7.2 48.4 %all-gather.4.cloned.1.call-start = ((), (), s32[]{:S(2)}) async-start(), calls=%async_computation | async-start | bytes 2621440 | tf_op jit(solution)/shard_map/all_gather | solution.py:41
  10.0 9.1 %copy-start.22 = (bf16[256,1024]{1,0:T(8,128)(2,1)S(1)}, bf16[256,1024]{1,0:T(8,128)(2,1)}, u32[]{:S(2)}) copy-start(bf16[256,1024]{1,0:T(8,128)(2,1)} %get-tuple-element.66.refs_0_) | copy-start | bytes 1572868
  10.0 86.7 %all-gather.6.cloned.1.call-start = ((), (), s32[]{:S(2)}) async-start(), calls=%async_computation.1 | async-start | bytes 4718592 | tf_op jit(solution)/shard_map/all_gather | solution.py:41
  16.2 140.1 %all-gather.8.cloned.1.call-start = ((), (), s32[]{:S(2)}) async-start(), calls=%async_computation.2 | async-start | bytes 5242880 | tf_op jit(solution)/shard_map/all_gather | solution.py:41
  16.3 5.5 %collective-permute-start = (bf16[8,256,512]{2,1,0:T(8,128)(2,1)}, bf16[8,256,512]{2,1,0:T(8,128)(2,1)S(1)}, u32[]{:S(2)}, u32[]{:S(2)}) collective-permute-start(bf16[8,256,512]{2,1,0:T(8,128)(2,1)} %get-tuple-element.46), channel_id=1, source_target_pairs={{0,1},{1,0},{2,3},{3,2},{4,5},{5,4},{6,7},{7,6},{8,9},{9,8},{10,11... | collective-permute-start | bytes 6291464 | tf_op jit(solution)/shard_map/ppermute | solution.py:29
  17.8 13.8 %collective-permute-start.5 = (bf16[512,512]{1,0:T(8,128)(2,1)}, bf16[512,512]{1,0:T(8,128)(2,1)S(1)}, u32[]{:S(2)}, u32[]{:S(2)}) collective-permute-start(bf16[512,512]{1,0:T(8,128)(2,1)} %get-tuple-element.67), channel_id=1, source_target_pairs={{0,64},{16,80},{32,96},{48,112},{64,0},{80,16},{96,32},{112,48},{1... | collective-permute-start | bytes 1572872 | tf_op jit(solution)/shard_map/ppermute | solution.py:37
  19.1 25.9 %collective-permute-start.4 = (bf16[256,1024]{1,0:T(8,128)(2,1)S(1)}, bf16[256,1024]{1,0:T(8,128)(2,1)S(1)}, u32[]{:S(2)}, u32[]{:S(2)}) collective-permute-start(bf16[256,1024]{1,0:T(8,128)(2,1)S(1)} %copy-done.22), channel_id=1, source_target_pairs={{0,2},{1,3},{2,0},{3,1},{4,6},{5,7},{6,4},{7,5},{8,10},{9,11},{10,... | collective-permute-start | bytes 1572872 | tf_op jit(solution)/shard_map/ppermute | solution.py:29
  21.8 1.3 copy-start.7
  26.3 26.6 %collective-permute-start.1 = (bf16[512,512]{1,0:T(8,128)(2,1)}, bf16[512,512]{1,0:T(8,128)(2,1)S(1)}, u32[]{:S(2)}, u32[]{:S(2)}) collective-permute-start(bf16[512,512]{1,0:T(8,128)(2,1)} %get-tuple-element.61), channel_id=1, source_target_pairs={{0,4},{1,5},{2,6},{3,7},{4,8},{5,9},{6,10},{7,11},{8,12},{9,13},{1... | collective-permute-start | bytes 1572872 | tf_op jit(solution)/shard_map/ppermute | solution.py:29
  27.8 29.9 %copy-start.35 = (s32[4]{0:T(128)S(1)}, s32[4]{0:T(128)}, u32[]{:S(2)}) copy-start(s32[4]{0:T(128)} %refs_0_.3) | copy-start | bytes 52
  27.8 30.0 %copy-start.25 = (bf16[512,512]{1,0:T(8,128)(2,1)S(1)}, bf16[512,512]{1,0:T(8,128)(2,1)}, u32[]{:S(2)}) copy-start(bf16[512,512]{1,0:T(8,128)(2,1)} %get-tuple-element.63) | copy-start | bytes 1572868
  27.8 25.2 %collective-permute-start.2 = (bf16[512,512]{1,0:T(8,128)(2,1)}, bf16[512,512]{1,0:T(8,128)(2,1)S(1)}, u32[]{:S(2)}, u32[]{:S(2)}) collective-permute-start(bf16[512,512]{1,0:T(8,128)(2,1)} %get-tuple-element.62), channel_id=1, source_target_pairs={{0,12},{1,13},{2,14},{3,15},{4,0},{5,1},{6,2},{7,3},{8,4},{9,5},{1... | collective-permute-start | bytes 1572872 | tf_op jit(solution)/shard_map/ppermute | solution.py:29
  31.6 24.0 %copy-start.18 = (bf16[512,512]{1,0:T(8,128)(2,1)}, bf16[512,512]{1,0:T(8,128)(2,1)S(1)}, u32[]{:S(2)}) copy-start(bf16[512,512]{1,0:T(8,128)(2,1)S(1)} %collective-permute-done.5.refs_3_) | copy-start | bytes 1572868
  45.0 8.0 %copy-start.23 = (bf16[256,1024]{1,0:T(8,128)(2,1)}, bf16[256,1024]{1,0:T(8,128)(2,1)S(1)}, u32[]{:S(2)}) copy-start(bf16[256,1024]{1,0:T(8,128)(2,1)S(1)} %collective-permute-done.4.refs_1_) | copy-start | bytes 1572868
  53.0 2.6 %copy-start.8 = (bf16[512,512]{1,0:T(8,128)(2,1)}, bf16[512,512]{1,0:T(8,128)(2,1)S(1)}, u32[]{:S(2)}) copy-start(bf16[512,512]{1,0:T(8,128)(2,1)S(1)} %collective-permute-done.1.refs_4_.refs_1_) | copy-start | bytes 1572868
  53.0 2.6 %copy-start.9 = (bf16[512,512]{1,0:T(8,128)(2,1)}, bf16[512,512]{1,0:T(8,128)(2,1)S(1)}, u32[]{:S(2)}) copy-start(bf16[512,512]{1,0:T(8,128)(2,1)S(1)} %collective-permute-done.2.refs_5_.refs_2_) | copy-start | bytes 1572868
  57.8 15.0 %collective-permute-start.3 = (bf16[512,512]{1,0:T(8,128)(2,1)S(1)}, bf16[512,512]{1,0:T(8,128)(2,1)S(1)}, u32[]{:S(2)}, u32[]{:S(2)}) collective-permute-start(bf16[512,512]{1,0:T(8,128)(2,1)S(1)} %copy-done.25), channel_id=1, source_target_pairs={{0,8},{1,9},{2,10},{3,11},{4,12},{5,13},{6,14},{7,15},{8,0},{9,1},... | collective-permute-start | bytes 1572872 | tf_op jit(solution)/shard_map/ppermute | solution.py:29
  61.0 14.1 %collective-permute-start.6 = (f32[512,256]{1,0:T(8,128)S(1)}, f32[512,256]{1,0:T(8,128)S(1)}, u32[]{:S(2)}, u32[]{:S(2)}) collective-permute-start(f32[512,256]{1,0:T(8,128)S(1)} %constant_dynamic-slice_fusion.2), channel_id=1, source_target_pairs={{0,32},{16,48},{32,0},{48,16},{64,96},{80,112},{96,64},{112,80},{1... | collective-permute-start | bytes 1572872 | tf_op jit(solution)/shard_map/ppermute | solution.py:37
  63.9 47.3 %collective-permute-start.7 = (bf16[1024,1024]{1,0:T(8,128)(2,1)}, bf16[1024,1024]{1,0:T(8,128)(2,1)}, u32[]{:S(2)}, u32[]{:S(2)}) collective-permute-start(bf16[1024,1024]{1,0:T(8,128)(2,1)} %get-tuple-element.73), channel_id=1, source_target_pairs={{0,2},{1,3},{2,0},{3,1},{4,6},{5,7},{6,4},{7,5},{8,10},{9,11},{10,... | collective-permute-start | bytes 6291464 | tf_op jit(solution)/shard_map/ppermute | solution.py:29
  72.8 2.3 %copy-start.24 = (bf16[512,512]{1,0:T(8,128)(2,1)}, bf16[512,512]{1,0:T(8,128)(2,1)S(1)}, u32[]{:S(2)}) copy-start(bf16[512,512]{1,0:T(8,128)(2,1)S(1)} %collective-permute-done.3.refs_3_) | copy-start | bytes 1572868
  75.1 0.8 copy-start.12
  75.9 10.0 %copy-start.32 = (f32[512,128]{1,0:T(8,128)S(1)}, f32[512,128]{1,0:T(8,128)}, u32[]{:S(2)}) copy-start(f32[512,128]{1,0:T(8,128)} %param.11) | copy-start | bytes 786436
  78.4 2.2 %copy-start.11 = (bf16[512,512]{1,0:T(8,128)(2,1)S(1)}, bf16[512,512]{1,0:T(8,128)(2,1)}, u32[]{:S(2)}) copy-start(bf16[512,512]{1,0:T(8,128)(2,1)} %get-tuple-element.78) | copy-start | bytes 1572868
  79.7 6.2 %collective-permute-start.15 = (f32[512,128]{1,0:T(8,128)S(1)}, f32[512,128]{1,0:T(8,128)S(1)}, u32[]{:S(2)}, u32[]{:S(2)}) collective-permute-start(f32[512,128]{1,0:T(8,128)S(1)} %constant_dynamic-slice_fusion), channel_id=1, source_target_pairs={{0,16},{16,0},{32,48},{48,32},{64,80},{80,64},{96,112},{112,96},{1... | collective-permute-start | bytes 786440 | tf_op jit(solution)/shard_map/ppermute | solution.py:37
  80.6 25.1 %collective-permute-start.12 = (bf16[512,512]{1,0:T(8,128)(2,1)S(1)}, bf16[512,512]{1,0:T(8,128)(2,1)S(1)}, u32[]{:S(2)}, u32[]{:S(2)}) collective-permute-start(bf16[512,512]{1,0:T(8,128)(2,1)S(1)} %copy-done.11), channel_id=1, source_target_pairs={{0,4},{1,5},{2,6},{3,7},{4,8},{5,9},{6,10},{7,11},{8,12},{9,13},{1... | collective-permute-start | bytes 1572872 | tf_op jit(solution)/shard_map/ppermute | solution.py:29
  81.4 24.4 %collective-permute-start.13 = (bf16[512,512]{1,0:T(8,128)(2,1)}, bf16[512,512]{1,0:T(8,128)(2,1)}, u32[]{:S(2)}, u32[]{:S(2)}) collective-permute-start(bf16[512,512]{1,0:T(8,128)(2,1)} %get-tuple-element.79), channel_id=1, source_target_pairs={{0,12},{1,13},{2,14},{3,15},{4,0},{5,1},{6,2},{7,3},{8,4},{9,5},{1... | collective-permute-start | bytes 1572872 | tf_op jit(solution)/shard_map/ppermute | solution.py:29
  87.6 13.0 %copy-start.20 = (f32[512,128]{1,0:T(8,128)}, f32[512,128]{1,0:T(8,128)S(1)}, u32[]{:S(2)}) copy-start(f32[512,128]{1,0:T(8,128)S(1)} %get-tuple-element.84.refs_0_) | copy-start | bytes 786436
  87.6 44.8 %collective-permute-start.16 = (f32[512,128]{1,0:T(8,128)S(1)}, f32[512,128]{1,0:T(8,128)}, u32[]{:S(2)}, u32[]{:S(2)}) collective-permute-start(f32[512,128]{1,0:T(8,128)S(1)} %get-tuple-element.84.refs_0_), channel_id=1, source_target_pairs={{0,64},{16,80},{32,96},{48,112},{64,0},{80,16},{96,32},{112,48},{1... | collective-permute-start | bytes 786440 | tf_op jit(solution)/shard_map/ppermute | solution.py:37
  96.7 6.8 %copy-start.33 = (bf16[2048,1024]{1,0:T(8,128)(2,1)S(1)}, bf16[2048,1024]{1,0:T(8,128)(2,1)}, u32[]{:S(2)}) copy-start(bf16[2048,1024]{1,0:T(8,128)(2,1)} %all-gather.6.cloned.1.call-done) | copy-start | bytes 12582916
  96.7 6.8 %copy-start.37 = (bf16[2048,256]{1,0:T(8,128)(2,1)S(1)}, bf16[2048,256]{1,0:T(8,128)(2,1)}, u32[]{:S(2)}) copy-start(bf16[2048,256]{1,0:T(8,128)(2,1)} %get-tuple-element.71) | copy-start | bytes 3145732
  100.6 5.1 %copy-start.4 = (f32[256,1024]{1,0:T(8,128)}, f32[256,1024]{1,0:T(8,128)S(1)}, u32[]{:S(2)}) copy-start(f32[256,1024]{1,0:T(8,128)S(1)} %fusion.12.refs_2_.refs_3_) | copy-start | bytes 3145732
  100.6 38.5 %collective-permute-start.17 = (f32[256,1024]{1,0:T(8,128)S(1)}, f32[256,1024]{1,0:T(8,128)S(1)}, u32[]{:S(2)}, u32[]{:S(2)}) collective-permute-start(f32[256,1024]{1,0:T(8,128)S(1)} %fusion.12.refs_2_.refs_3_), channel_id=1, source_target_pairs={{0,2},{1,3},{2,0},{3,1},{4,6},{5,7},{6,4},{7,5},{8,10},{9,11},{10,... | collective-permute-start | bytes 3145736 | tf_op jit(solution)/shard_map/ppermute | solution.py:29
  105.8 0.8 copy-start.19
  106.6 4.6 %copy-start.21 = (bf16[256,1024]{1,0:T(8,128)(2,1)S(1)}, bf16[256,1024]{1,0:T(8,128)(2,1)}, u32[]{:S(2)}) copy-start(bf16[256,1024]{1,0:T(8,128)(2,1)} %refs_2_.1) | copy-start | bytes 1572868
  106.6 25.9 %collective-permute-start.14 = (bf16[512,512]{1,0:T(8,128)(2,1)}, bf16[512,512]{1,0:T(8,128)(2,1)S(1)}, u32[]{:S(2)}, u32[]{:S(2)}) collective-permute-start(bf16[512,512]{1,0:T(8,128)(2,1)} %last_cols.1), channel_id=1, source_target_pairs={{0,8},{1,9},{2,10},{3,11},{4,12},{5,13},{6,14},{7,15},{8,0},{9,1},... | collective-permute-start | bytes 1572872 | tf_op jit(solution)/shard_map/ppermute | solution.py:29
  109.7 10.2 %copy-start.27 = (bf16[256,1024]{1,0:T(8,128)(2,1)}, bf16[256,1024]{1,0:T(8,128)(2,1)S(1)}, u32[]{:S(2)}) copy-start(bf16[256,1024]{1,0:T(8,128)(2,1)S(1)} %constant_dynamic-slice_fusion.1) | copy-start | bytes 1572868
  114.2 5.6 %copy-start.13 = (bf16[1024,1024]{1,0:T(8,128)(2,1)S(1)}, bf16[1024,1024]{1,0:T(8,128)(2,1)}, u32[]{:S(2)}) copy-start(bf16[1024,1024]{1,0:T(8,128)(2,1)} %get-tuple-element.73) | copy-start | bytes 6291460
  115.3 13.8 %collective-permute-start.11 = (bf16[256,1024]{1,0:T(8,128)(2,1)}, bf16[256,1024]{1,0:T(8,128)(2,1)S(1)}, u32[]{:S(2)}, u32[]{:S(2)}) collective-permute-start(bf16[256,1024]{1,0:T(8,128)(2,1)} %get-tuple-element.88), channel_id=1, source_target_pairs={{0,1},{1,0},{2,3},{3,2},{4,5},{5,4},{6,7},{7,6},{8,9},{9,8},{10,11... | collective-permute-start | bytes 1572872 | tf_op jit(solution)/shard_map/ppermute | solution.py:29
  122.2 6.9 %collective-permute-start.10 = (bf16[256,1024]{1,0:T(8,128)(2,1)}, bf16[256,1024]{1,0:T(8,128)(2,1)}, u32[]{:S(2)}, u32[]{:S(2)}) collective-permute-start(bf16[256,1024]{1,0:T(8,128)(2,1)} %get-tuple-element.90), channel_id=1, source_target_pairs={{0,1},{1,0},{2,3},{3,2},{4,5},{5,4},{6,7},{7,6},{8,9},{9,8},{10,11... | collective-permute-start | bytes 1572872 | tf_op jit(solution)/shard_map/ppermute | solution.py:29
  123.1 3.3 %copy-start.3 = (bf16[512,1024]{1,0:T(8,128)(2,1)S(1)}, bf16[512,1024]{1,0:T(8,128)(2,1)}, u32[]{:S(2)}) copy-start(bf16[512,1024]{1,0:T(8,128)(2,1)} %get-tuple-element.72) | copy-start | bytes 3145732
  123.1 3.3 %copy-start.14 = (bf16[1024,1024]{1,0:T(8,128)(2,1)S(1)}, bf16[1024,1024]{1,0:T(8,128)(2,1)}, u32[]{:S(2)}) copy-start(bf16[1024,1024]{1,0:T(8,128)(2,1)} %get-tuple-element.73) | copy-start | bytes 6291460
  129.0 0.8 copy-start.26
  132.4 6.7 %copy-start.10 = (bf16[512,512]{1,0:T(8,128)(2,1)}, bf16[512,512]{1,0:T(8,128)(2,1)S(1)}, u32[]{:S(2)}) copy-start(bf16[512,512]{1,0:T(8,128)(2,1)S(1)} %collective-permute-done.14.refs_4_.refs_3_) | copy-start | bytes 1572868
  139.2 1.0 copy-start.1
  141.9 25.6 %collective-permute-start.19 = (f32[512,256]{1,0:T(8,128)}, f32[512,256]{1,0:T(8,128)S(1)}, u32[]{:S(2)}, u32[]{:S(2)}) collective-permute-start(f32[512,256]{1,0:T(8,128)} %get-tuple-element.83.refs_0_), channel_id=1, source_target_pairs={{0,16},{16,32},{32,48},{48,0},{64,80},{80,96},{96,112},{112,64},{1... | collective-permute-start | bytes 1572872 | tf_op jit(solution)/shard_map/ppermute | solution.py:309
  142.9 30.0 %collective-permute-start.20 = (f32[512,256]{1,0:T(8,128)}, f32[512,256]{1,0:T(8,128)S(1)}, u32[]{:S(2)}, u32[]{:S(2)}) collective-permute-start(f32[512,256]{1,0:T(8,128)} %get-tuple-element.83.refs_0_), channel_id=1, source_target_pairs={{0,48},{16,0},{32,16},{48,32},{64,112},{80,64},{96,80},{112,96},{1... | collective-permute-start | bytes 1572872 | tf_op jit(solution)/shard_map/ppermute | solution.py:309
  144.7 28.3 %collective-permute-start.21 = (f32[512,256]{1,0:T(8,128)}, f32[512,256]{1,0:T(8,128)S(1)}, u32[]{:S(2)}, u32[]{:S(2)}) collective-permute-start(f32[512,256]{1,0:T(8,128)} %get-tuple-element.83.refs_0_), channel_id=1, source_target_pairs={{0,32},{16,48},{32,0},{48,16},{64,96},{80,112},{96,64},{112,80},{1... | collective-permute-start | bytes 1572872 | tf_op jit(solution)/shard_map/ppermute | solution.py:309
  144.8 35.4 %collective-permute-start.18 = (f32[256,1024]{1,0:T(8,128)}, f32[256,1024]{1,0:T(8,128)}, u32[]{:S(2)}, u32[]{:S(2)}) collective-permute-start(f32[256,1024]{1,0:T(8,128)} %get-tuple-element.82.refs_4_), channel_id=1, source_target_pairs={{0,2},{1,3},{2,0},{3,1},{4,6},{5,7},{6,4},{7,5},{8,10},{9,11},{10,... | collective-permute-start | bytes 3145736 | tf_op jit(solution)/shard_map/ppermute | solution.py:29
  147.7 8.6 %copy-start.28 = (bf16[256,1024]{1,0:T(8,128)(2,1)S(1)}, bf16[256,1024]{1,0:T(8,128)(2,1)}, u32[]{:S(2)}) copy-start(bf16[256,1024]{1,0:T(8,128)(2,1)} %copy-done.27) | copy-start | bytes 1572868
  156.3 6.9 %copy-start.36 = (bf16[2048,1024]{1,0:T(8,128)(2,1)S(1)}, bf16[2048,1024]{1,0:T(8,128)(2,1)}, u32[]{:S(2)}) copy-start(bf16[2048,1024]{1,0:T(8,128)(2,1)} %all-gather.8.cloned.1.call-done) | copy-start | bytes 12582916
  161.0 2.4 %copy-start.5 = (f32[512,1024]{1,0:T(8,128)S(1)}, f32[512,1024]{1,0:T(8,128)}, u32[]{:S(2)}) copy-start(f32[512,1024]{1,0:T(8,128)} %convolution_add_fusion.1.refs_5_) | copy-start | bytes 6291460
  161.0 3.0 %copy-start.6 = (bf16[512,2048]{1,0:T(8,128)(2,1)S(1)}, bf16[512,2048]{1,0:T(8,128)(2,1)}, u32[]{:S(2)}) copy-start(bf16[512,2048]{1,0:T(8,128)(2,1)} %get-tuple-element.75) | copy-start | bytes 6291460
  162.7 24.2 %collective-permute-start.9 = (bf16[256,2048]{1,0:T(8,128)(2,1)}, bf16[256,2048]{1,0:T(8,128)(2,1)}, u32[]{:S(2)}, u32[]{:S(2)}) collective-permute-start(bf16[256,2048]{1,0:T(8,128)(2,1)} %get-tuple-element.86), channel_id=1, source_target_pairs={{0,1},{1,0},{2,3},{3,2},{4,5},{5,4},{6,7},{7,6},{8,9},{9,8},{10,11... | collective-permute-start | bytes 3145736 | tf_op jit(solution)/shard_map/ppermute | solution.py:29
  164.0 5.0 %copy-start.34 = (bf16[2048,1024]{1,0:T(8,128)(2,1)S(1)}, bf16[2048,1024]{1,0:T(8,128)(2,1)}, u32[]{:S(2)}) copy-start(bf16[2048,1024]{1,0:T(8,128)(2,1)} %all-gather.6.cloned.1.call-done) | copy-start | bytes 12582916
  166.4 6.6 %copy-start.15 = (f32[512,1024]{1,0:T(8,128)}, f32[512,1024]{1,0:T(8,128)S(1)}, u32[]{:S(2)}) copy-start(f32[512,1024]{1,0:T(8,128)S(1)} %convolution_add_fusion) | copy-start | bytes 6291460
  166.4 2.9 %copy-start.17 = (bf16[2048,512]{1,0:T(8,128)(2,1)S(1)}, bf16[2048,512]{1,0:T(8,128)(2,1)}, u32[]{:S(2)}) copy-start(bf16[2048,512]{1,0:T(8,128)(2,1)} %line_own.1) | copy-start | bytes 6291460
  167.5 5.4 %copy-start.29 = (f32[512,256]{1,0:T(8,128)}, f32[512,256]{1,0:T(8,128)S(1)}, u32[]{:S(2)}) copy-start(f32[512,256]{1,0:T(8,128)S(1)} %collective-permute-done.19.refs_1_) | copy-start | bytes 1572868
  167.5 17.2 %collective-permute-start.8 = (f32[256,1024]{1,0:T(8,128)}, f32[256,1024]{1,0:T(8,128)}, u32[]{:S(2)}, u32[]{:S(2)}) collective-permute-start(f32[256,1024]{1,0:T(8,128)} %slice.37), channel_id=1, source_target_pairs={{0,1},{1,0},{2,3},{3,2},{4,5},{5,4},{6,7},{7,6},{8,9},{9,8},{10,11... | collective-permute-start | bytes 3145736 | tf_op jit(solution)/shard_map/ppermute | solution.py:29
  173.0 0.8 copy-start.30
  173.8 0.8 copy-start.31
  180.2 1.6 copy-start
  180.2 1.9 copy-start.2
  182.0 2.7 %copy-start.16 = (f32[512,1024]{1,0:T(8,128)S(1)}, f32[512,1024]{1,0:T(8,128)}, u32[]{:S(2)}) copy-start(f32[512,1024]{1,0:T(8,128)} %copy-done.15) | copy-start | bytes 6291460
Sparse Core Ops, SparseCore 0:
  10.2 45.2 all-gather.3
  57.2 39.3 all-gather.5
  98.4 57.8 all-gather.7

commit v2 on v1

--- a/solution.py
+++ b/solution.py
@@ -130,7 +130,7 @@
     return jax.ShapeDtypeStruct(shape, jnp.bfloat16)
 
 
-def place_columns(parts, width, into=None):
+def place_columns(parts, width, into=None, deps=()):
     rows = parts[0][0].shape[0]
     srcs = [p[0] for p in parts]
     last = 0
@@ -145,7 +145,7 @@
         return jobs
 
     outs, keep = ([bf16(rows, width)], []) if into is None else ([], [into])
-    return move("place_columns", srcs, outs, plan, keep=keep)[0]
+    return move("place_columns", srcs, outs, plan, keep=keep, deps=deps)[0]
 
 
 def split_half(total, here):
@@ -219,15 +219,21 @@
 
     l1, r1, o1 = send(s1[1], y_shift(1)), send(s1[3], y_shift(-1)), send(s1[2], y_shift(2))
 
-    wa_pair, wb_line, came = move(
+    upper, lower = pl.ds(0, BLOCK), pl.ds(BLOCK, BLOCK)
+    wa_pair, wb_upper, wb_lower, came = move(
         "a_pair",
-        [wa, wa_x],
-        [bf16(BLOCK, cols)],
-        lambda *_: [(0, (top,), half, [(0, (top,), None)]), (1, (top,), half, [(0, (low,), None)])],
-        keep=[wb_line, came],
+        [wa, wa_x, wb_line],
+        [bf16(BLOCK, cols)] * 3,
+        lambda *_: [
+            (2, (upper,), (BLOCK, cols), [(1, (every,), None)]),
+            (2, (lower,), (BLOCK, cols), [(2, (every,), None)]),
+            (0, (top,), half, [(0, (top,), None)]),
+            (1, (top,), half, [(0, (low,), None)]),
+        ],
+        keep=[came],
         deps=[l1, r1],
     )
-    wb_line_x = send(wb_line, X_SWAP)
+    wb_upper_x = send(wb_upper, X_SWAP)
     wa_line = line_gather(wa_pair, LINES)
 
     synced = lax.dynamic_index_in_dim(weights[0], fragment[0], 0, keepdims=False)
@@ -239,7 +245,7 @@
     came = rep_swap(away, 2)
 
     line = tuple(enumerate((0, -1, 1, 2)))
-    line1_top, line1_low, s0[1], s0[3], came = move(
+    line1_top, line1_low, s0[1], s0[3], came, wb_lower = move(
         "line_across",
         [s1[0], l1, r1, o1],
         [bf16(NY * BLOCK, HALF)] * 2,
@@ -252,8 +258,10 @@
             )
             for n, dy in line
         ],
-        keep=[s0[1], s0[3], came],
-    )
+        keep=[s0[1], s0[3], came, wb_lower],
+        deps=[wb_upper_x],
+    )
+    wb_lower_x = send(wb_lower, X_SWAP)
     l0, r0 = send(s0[1], y_shift(1)), send(s0[3], y_shift(-1))
     total, away = split_half(total + came, z_lo)
     total = total + rep_swap(away, 1)
@@ -280,10 +288,17 @@
 
         return plan
 
-    x_b = move("after_part", [], [], None, keep=x_b, deps=[part1_top, part1_low])
-
     (s0[2],) = move("last_cols", [], [], None, keep=[s0[2]], deps=[l0, r0, part1_top, part1_low])
     o0 = send(s0[2], y_shift(2))
+    wb_line_x, *x_b = move(
+        "after_part",
+        [wb_upper_x, wb_lower_x],
+        [bf16(2 * BLOCK, cols)],
+        lambda *_: [(i, (every,), (BLOCK, cols), [(0, (cut,), None)]) for i, cut in enumerate((upper, lower))],
+        keep=x_b,
+        deps=[part1_top, part1_low, s0[2]],
+    )
+
     g_beside = lax.dynamic_slice_in_dim(g_line, y * BLOCK + (1 - core) * HALF, HALF, 0)
     g_pair = jnp.concatenate([grad_values, g_beside], 0)
 
@@ -296,34 +311,6 @@
 
     v_b1, gx_b1 = both(x_b[1], wb_line_x, [(yy, 1, 1) for yy in range(NY)])
     v_b = v_b0 + v_b1
-
-    found, part1_low = move(
-        "last_part",
-        [found, came],
-        [f32(2)],
-        beside(1, lambda spot: spot.x_lo),
-        keep=[part1_low],
-        deps=[part1_top_x, o0, v_b, gx_b0[0][0], gx_b1[0][0]],
-    )
-    part1_low_x = send(part1_low, X_SWAP)
-    shares = [found] + [lax.ppermute(found, "rep", z_shift(d)) for d in (1, -1, 2)]
-
-    v_a, gx_a = both(x_a, wa_line, [(yy, dx, 0) for yy in range(NY) for dx in range(2)])
-    v = v_b + v_a
-
-    def anchor_columns(spot, _):
-        return [
-            (i, blocks(xx), (BLOCK, share_cols), [(0, blocks(xx * 4 + (spot.z + dz) % 4), None)])
-            for i, dz in enumerate((0, 3, 1, 2))
-            for xx in range(2)
-        ]
-
-    (new_anchor,) = move("anchor_columns", shares, [f32(8)], anchor_columns)
-    blended = (mix_weight * synced.astype(jnp.float32) + (1.0 - mix_weight) * new_anchor).astype(jnp.bfloat16)
-
-    values = (v[:HALF] + send(v[HALF:], CORE_SWAP)).astype(jnp.bfloat16)
-    token_grad = place_columns(gx_b0 + gx_b1, tokens.shape[1])
-    token_grad = place_columns(gx_a, tokens.shape[1], token_grad)
 
     (line0,) = move(
         "line_own",
@@ -332,9 +319,47 @@
         lambda spot, _: [
             (n, (every,), (BLOCK, BLOCK), [(0, (at(spot.row(dy) * BLOCK, BLOCK),), None)]) for n, dy in line
         ],
-        deps=[part1_low],
+        deps=[v_b],
     )
     part0 = wide_dot(line0, g_line, ((0,), (0,)))
+
+    found, part1_low = move(
+        "last_part",
+        [found, came],
+        [f32(2)],
+        beside(1, lambda spot: spot.x_lo),
+        keep=[part1_low],
+        deps=[part1_top_x, part0, gx_b0[0][0], gx_b1[0][0]],
+    )
+    part1_low_x = send(part1_low, X_SWAP)
+    shares = [found] + [lax.ppermute(found, "rep", z_shift(d)) for d in (1, -1, 2)]
+
+    (wa_line,) = move("a_line", [], [], None, keep=[wa_line], deps=[part1_low])
+    pieces_a = [(yy, dx, 0) for yy in range(NY) for dx in range(2)]
+
+    def a_products(rows_of):
+        gx = wide_dot(g_pair[rows_of], wa_line, ((1,), (1,))).astype(jnp.bfloat16)
+        return gx, v_b[rows_of] + wide_dot(x_a[rows_of], wa_line, ((1,), (0,)))
+
+    gx_other, v_other = a_products(slice(HALF, None))
+    gx_other, v_other = send(gx_other, CORE_SWAP), send(v_other, CORE_SWAP)
+    gx_mine, v_mine = a_products(slice(0, HALF))
+    gx_a = [(gx_mine, 0, pieces_a), (gx_other, 1, pieces_a)]
+
+    def anchor_columns(spot, _):
+        return [
+            (i, blocks(xx), (BLOCK, share_cols), [(0, blocks(xx * 4 + (spot.z + dz) % 4), None)])
+            for i, dz in enumerate((0, 3, 1, 2))
+            for xx in range(2)
+        ]
+
+    (new_anchor,) = move("anchor_columns", shares, [f32(8)], anchor_columns, deps=[gx_mine, v_mine])
+    blended = (mix_weight * synced.astype(jnp.float32) + (1.0 - mix_weight) * new_anchor).astype(jnp.bfloat16)
+
+    values = (v_mine + v_other).astype(jnp.bfloat16)
+    token_grad = place_columns(gx_b0 + gx_b1, tokens.shape[1], deps=[part1_low])
+    token_grad = place_columns(gx_a, tokens.shape[1], token_grad)
+
     (part1_low_x,) = move("rest", [], [], None, keep=[part1_low_x], deps=[part0, new_anchor])
     grad_weight = (part0 + jnp.concatenate([part1_top_x, part1_low_x], 0)).astype(jnp.bfloat16)
 

time: 197 us -> 195 us (0.990)
  waiting for transfers between devices: 60.1 us -> 49.7 us
  matrix products: 27.2 us -> 32.7 us
  Pallas kernels: 28.5 us -> 31.9 us
  starting transfers between devices: 38 us -> 40.3 us
    all_gather x3, waiting for transfers between devices: 16.9 us -> 2.58 us  [line_gather(): lax.all_gather(x, 'shard', axis=0, tiled=True, axis_index_groups=groups)]
    dot_general x9 -> x11, matrix products: 27.2 us -> 32.7 us  [wide_dot(): lax.dot_general(a, b, (dims, ((), ())), preferred_element_type=jnp.float32)]
    ppermute x4, waiting for transfers between devices: 7.1 us -> 11.4 us  [rep_swap(): return lax.ppermute(x, 'rep', [(r, r ^ bit) for r in range(8)])]
    pallas_call x13 -> x14, Pallas kernels: 28.5 us -> 31.9 us  [move(): pl.pallas_call(body, out_shape=[jax.ShapeDtypeStruct(o.shape, o.dtype) fo...]
    ppermute x15 -> x16, starting transfers between devices: 29 us -> 30.6 us  [send(): return lax.ppermute(x, 'shard', pairs)]
    unnamed x76 -> x74, local copies, waits for them, and re-layouts: 9.31 us -> 10.3 us
    ppermute x15 -> x16, waiting for transfers between devices: 36.1 us -> 35.7 us  [send(): return lax.ppermute(x, 'shard', pairs)]
  transfers between devices with their start and end apart: 25 -> 26, of which waited for: 12 -> 8; matrix products, arithmetic and copies ran while one was open for 23% -> 24% of each run, Pallas kernels for 12% -> 14%
where the time goes in v2:
time: 195 us; the launch traced here: 193 us
  waiting for transfers between devices  49.7 us (25%)
  starting transfers between devices  40.3 us (21%)
  matrix products  32.7 us (17%)
  Pallas kernels  31.9 us (16%)
  between operations  14.2 us (7%)
  local copies, waits for them, and re-layouts  13.6 us (7%)
  other arithmetic  10.6 us (5%)
    ppermute x16, waiting for transfers between devices, send(): return lax.ppermute(x, 'shard', pairs)  35.7 us
    dot_general x11, matrix products, wide_dot(): lax.dot_general(a, b, (dims, ((), ())), preferred_element_type=jnp.float32)  32.7 us
    pallas_call x14, Pallas kernels, move(): pl.pallas_call(body, out_shape=[jax.ShapeDtypeStruct(o.shape, o.dtype) fo...  31.9 us
    ppermute x16, starting transfers between devices, send(): return lax.ppermute(x, 'shard', pairs)  30.6 us
    ppermute x4, waiting for transfers between devices, rep_swap(): return lax.ppermute(x, 'rep', [(r, r ^ bit) for r in range(8)])  11.4 us
    unnamed x74, local copies, waits for them, and re-layouts  10.3 us
    ppermute x4, starting transfers between devices, rep_swap(): return lax.ppermute(x, 'rep', [(r, r ^ bit) for r in range(8)])  5.48 us
    ppermute x3, starting transfers between devices, local(): lax.ppermute(found, 'rep', z_shift(d))  4.15 us
  transfers between devices with their start and end apart: 26, of which 8 were waited for; matrix products, arithmetic and copies ran while one was open for 24% of the time, Pallas kernels for 14%

profile of v2, /device:TPU:1, one launch (start us, length us, event | category | flops | bytes accessed | tf_op | source)
XLA Modules:
  0.0 193.1 jit_solution(11283467464245233777)
XLA Ops:
  7.2 2.7 %pick_rows.1 = (bf16[256,1024]{1,0:T(8,128)(2,1)}, bf16[256,1024]{1,0:T(8,128)(2,1)}) custom-call(s32[4]{0:T(128)} %refs_0_.3, bf16[1,4,512,1024]{3,2,1,0:T(8,128)(2,1)} %refs_3_.1), custom_call_target="tpu_custom_call" | custom-call | flops 1 | bytes 1 | tf_op jit(solution)/shard_map/pick_rows/pallas_call | solution.py:115
  10.0 6.2 %split_tokens.1 = (bf16[8,256,512]{2,1,0:T(8,128)(2,1)}, bf16[256,1024]{1,0:T(8,128)(2,1)}, bf16[512,512]{1,0:T(8,128)(2,1)}, bf16[512,512]{1,0:T(8,128)(2,1)}, ...) custom-call(s32[4]{0:T(128)} %refs_0_.3, ...), custom_call_target="tpu_custom_call" | custom-call | flops 1 | bytes 1 | tf_op jit(solution)/shard_map/split_tokens/pallas_call | solution.py:115
  16.3 1.5 collective-permute-start.2
  17.8 2.8 %collective-permute-start = (bf16[256,1024]{1,0:T(8,128)(2,1)S(1)}, bf16[256,1024]{1,0:T(8,128)(2,1)}, u32[]{:S(2)}, u32[]{:S(2)}) collective-permute-start(bf16[256,1024]{1,0:T(8,128)(2,1)S(1)} %copy-done.28), channel_id=1, source_target_pairs={{0,2},{1,3},{2,0},{3,1},{4,6},{5,7},{6,4},{7,5},{8,10},{9,11},{10,... | collective-permute-start | bytes 1572872 | tf_op jit(solution)/shard_map/ppermute | solution.py:29
  20.9 0.8 collective-permute-done.2.refs_0_
  21.8 1.3 copy-done.14
  23.1 3.2 %fill_tokens.1 = (bf16[512,512]{1,0:T(8,128)(2,1)}, bf16[512,512]{1,0:T(8,128)(2,1)}, bf16[512,512]{1,0:T(8,128)(2,1)}, bf16[512,512]{1,0:T(8,128)(2,1)}, bf16[5...) custom-call(bf16[8,256,512]{2,1,0:T(8,128)(2,1)} %copy-done.14, ...), custom_call_target="tpu_custom_call", output_to_operand_aliasing={{0}: (1, {}), {1}: (2, {}), {2}: (3, {}), {3}: (4, {}), {4}... | custom-call | flops 1 | bytes 1 | tf_op jit(solution)/shard_map/fill_tokens/pallas_call | solution.py:115
  26.3 1.5 collective-permute-start.3
  27.8 1.5 collective-permute-start.4
  29.3 3.6 %collective-permute-done.refs_1_ = bf16[256,1024]{1,0:T(8,128)(2,1)} collective-permute-done((bf16[256,1024]{1,0:T(8,128)(2,1)S(1)}, bf16[256,1024]{1,0:T(8,128)(2,1)}, u32[]{:S(2)}, u32[]{:S(2)}) %collective-permute-start) | collective-permute-done | bytes 524320 | tf_op jit(solution)/shard_map/ppermute | solution.py:29
  32.9 11.4 %collective-permute-done.1.refs_3_ = bf16[512,512]{1,0:T(8,128)(2,1)S(1)} collective-permute-done((bf16[512,512]{1,0:T(8,128)(2,1)}, bf16[512,512]{1,0:T(8,128)(2,1)S(1)}, u32[]{:S(2)}, u32[]{:S(2)}) %collective-permute-start.1) | collective-permute-done | bytes 524320 | tf_op jit(solution)/shard_map/ppermute | solution.py:37
  44.3 8.7 %collective-permute-done.3.refs_4_.refs_1_ = bf16[512,512]{1,0:T(8,128)(2,1)S(1)} collective-permute-done((bf16[512,512]{1,0:T(8,128)(2,1)}, bf16[512,512]{1,0:T(8,128)(2,1)S(1)}, u32[]{:S(2)}, u32[]{:S(2)}) %collective-permute-start.3) | collective-permute-done | bytes 524320 | tf_op jit(solution)/shard_map/ppermute | solution.py:29
  53.0 2.6 %all-gather.4.cloned.1.call-done.refs_2_ = bf16[1024,1024]{1,0:T(8,128)(2,1)} async-done(((bf16[256,1024]{1,0:T(8,128)(2,1)}), bf16[1024,1024]{1,0:T(8,128)(2,1)}) %all-gather.4.cloned.1.call-update) | async-done | bytes 2097168 | tf_op jit(solution)/shard_map/all_gather | solution.py:41
  55.5 3.0 %a_pair.1 = (bf16[512,1024]{1,0:T(8,128)(2,1)}, bf16[512,1024]{1,0:T(8,128)(2,1)}, bf16[512,1024]{1,0:T(8,128)(2,1)}, bf16[512,512]{1,0:T(8,128)(2,1)}) custom-call(bf16[256,1024]{1,0:T(8,128)(2,1)} %get-tuple-element.48.refs_0_, bf16[256,1024]{1,0:T(8,128)(2,1)} %collective-permute-done.refs_1_, ...), custom_call_target="tpu_custom_call", output_to_operand_aliasing={{3}: (3, {})} | custom-call | flops 1 | bytes 1 | tf_op jit(solution)/shard_map/a_pair/pallas_call | solution.py:115
  58.5 2.8 %collective-permute-start.5 = (bf16[512,1024]{1,0:T(8,128)(2,1)}, bf16[512,1024]{1,0:T(8,128)(2,1)S(1)}, u32[]{:S(2)}, u32[]{:S(2)}) collective-permute-start(bf16[512,1024]{1,0:T(8,128)(2,1)} %get-tuple-element.65), channel_id=1, source_target_pairs={{0,2},{1,3},{2,0},{3,1},{4,6},{5,7},{6,4},{7,5},{8,10},{9,11},{10,... | collective-permute-start | bytes 3145736 | tf_op jit(solution)/shard_map/ppermute | solution.py:29
  61.4 1.6 collective-permute-start.6
  63.0 1.5 convert_add_fusion.1
  64.6 3.0 %collective-permute-start.7 = (f32[512,256]{1,0:T(8,128)S(1)}, f32[512,256]{1,0:T(8,128)S(1)}, u32[]{:S(2)}, u32[]{:S(2)}) collective-permute-start(f32[512,256]{1,0:T(8,128)S(1)} %constant_dynamic-slice_fusion.2), channel_id=1, source_target_pairs={{0,32},{16,48},{32,0},{48,16},{64,96},{80,112},{96,64},{112,80},{1... | collective-permute-start | bytes 1572872 | tf_op jit(solution)/shard_map/ppermute | solution.py:37
  67.5 12.3 %collective-permute-done.6.refs_3_ = bf16[512,512]{1,0:T(8,128)(2,1)} collective-permute-done((bf16[512,512]{1,0:T(8,128)(2,1)}, bf16[512,512]{1,0:T(8,128)(2,1)}, u32[]{:S(2)}, u32[]{:S(2)}) %collective-permute-start.6) | collective-permute-done | bytes 524320 | tf_op jit(solution)/shard_map/ppermute | solution.py:29
  79.9 4.5 %collective-permute-done.5.refs_8_.refs_0_ = bf16[512,1024]{1,0:T(8,128)(2,1)S(1)} collective-permute-done((bf16[512,1024]{1,0:T(8,128)(2,1)}, bf16[512,1024]{1,0:T(8,128)(2,1)S(1)}, u32[]{:S(2)}, u32[]{:S(2)}) %collective-permute-start.5) | collective-permute-done | bytes 1048608 | tf_op jit(solution)/shard_map/ppermute | solution.py:29
  84.4 1.0 copy-done.10
  85.4 2.5 %line_across.1 = (bf16[2048,256]{1,0:T(8,128)(2,1)}, bf16[2048,256]{1,0:T(8,128)(2,1)}, bf16[512,512]{1,0:T(8,128)(2,1)}, bf16[512,512]{1,0:T(8,128)(2,1)}, f32[...) custom-call(bf16[512,512]{1,0:T(8,128)(2,1)} %get-tuple-element.66.r, ...), custom_call_target="tpu_custom_call", output_to_operand_aliasing={{2}: (4, {}), {3}: (5, {}), {4}: (6, {}), {5}: (7, {})} | custom-call | flops 1 | bytes 1 | tf_op jit(solution)/shard_map/line_across/pallas_call | solution.py:115
  87.9 1.2 dynamic-slice_add_fusion
  89.1 1.4 collective-permute-start.11
  90.5 2.7 %collective-permute-start.8 = (bf16[512,1024]{1,0:T(8,128)(2,1)}, bf16[512,1024]{1,0:T(8,128)(2,1)}, u32[]{:S(2)}, u32[]{:S(2)}) collective-permute-start(bf16[512,1024]{1,0:T(8,128)(2,1)} %get-tuple-element.72), channel_id=1, source_target_pairs={{0,2},{1,3},{2,0},{3,1},{4,6},{5,7},{6,4},{7,5},{8,10},{9,11},{10,... | collective-permute-start | bytes 3145736 | tf_op jit(solution)/shard_map/ppermute | solution.py:29
  93.2 2.7 %collective-permute-start.10 = (bf16[512,512]{1,0:T(8,128)(2,1)}, bf16[512,512]{1,0:T(8,128)(2,1)S(1)}, u32[]{:S(2)}, u32[]{:S(2)}) collective-permute-start(bf16[512,512]{1,0:T(8,128)(2,1)} %get-tuple-element.80), channel_id=1, source_target_pairs={{0,12},{1,13},{2,14},{3,15},{4,0},{5,1},{6,2},{7,3},{8,4},{9,5},{1... | collective-permute-start | bytes 1572872 | tf_op jit(solution)/shard_map/ppermute | solution.py:29
  95.9 1.7 multiply_subtract_fusion
  97.6 0.9 collective-permute-start.12
  98.5 3.9 %fusion.18.refs_3_.refs_4_ = f32[256,1024]{1,0:T(8,128)S(1)} fusion(bf16[2048,256]{1,0:T(8,128)(2,1)} %get-tuple-element.75, bf16[2048,1024]{1,0:T(8,128)(2,1)} %all-gather.6.cloned.1.call-done), kind=kOutput, calls=%fused_computation.33 | convolution fusion | flops 1073741824 | bytes 6291456 | tf_op jit(solution)/shard_map/dot_general | solution.py:45
  102.4 2.2 %collective-permute-start.13 = (f32[256,1024]{1,0:T(8,128)S(1)}, f32[256,1024]{1,0:T(8,128)S(1)}, u32[]{:S(2)}, u32[]{:S(2)}) collective-permute-start(f32[256,1024]{1,0:T(8,128)S(1)} %fusion.18.refs_3_.refs_4_), channel_id=1, source_target_pairs={{0,2},{1,3},{2,0},{3,1},{4,6},{5,7},{6,4},{7,5},{8,10},{9,11},{10,... | collective-permute-start | bytes 3145736 | tf_op jit(solution)/shard_map/ppermute | solution.py:29
  104.7 2.2 %fusion.19.refs_4_.refs_5_.refs_2_ = f32[256,1024]{1,0:T(8,128)} fusion(bf16[2048,256]{1,0:T(8,128)(2,1)S(1)} %copy-done.36, bf16[2048,1024]{1,0:T(8,128)(2,1)S(1)} %copy-done.33), kind=kOutput, calls=%fused_computation.34 | convolution fusion | flops 1073741824 | bytes 6291456 | tf_op jit(solution)/shard_map/dot_general | solution.py:45
  107.9 1.6 collective-permute-start.14
  109.5 5.7 %collective-permute-done.8.refs_1_ = bf16[512,1024]{1,0:T(8,128)(2,1)} collective-permute-done((bf16[512,1024]{1,0:T(8,128)(2,1)}, bf16[512,1024]{1,0:T(8,128)(2,1)}, u32[]{:S(2)}, u32[]{:S(2)}) %collective-permute-start.8) | collective-permute-done | bytes 1048608 | tf_op jit(solution)/shard_map/ppermute | solution.py:29
  115.2 2.6 %after_part.1 = (bf16[1024,1024]{1,0:T(8,128)(2,1)}, bf16[512,1024]{1,0:T(8,128)(2,1)}, bf16[512,1024]{1,0:T(8,128)(2,1)}) custom-call(bf16[512,1024]{1,0:T(8,128)(2,1)} %copy-done.10, bf16[512,1024]{1,0:T(8,128)(2,1)} %collective-permute-done.8.refs_1_, bf16[512,1024]{1,0:T(8,128)(2,1)} %get-tuple-element.73.refs_2_, ...), custom_call_target="tpu_custom_call", output_to_operand_aliasing={{1}: (2, {}), {2}: (3, {})} | custom-call | flops 1 | bytes 1 | tf_op jit(solution)/shard_map/after_part/pallas_call | solution.py:115
  117.8 1.1 constant_dynamic-slice_fusion
  118.9 3.1 %convolution_convert_fusion.3 = bf16[512,1024]{1,0:T(8,128)(2,1)S(1)} fusion(bf16[1024,1024]{1,0:T(8,128)(2,1)} %all-gather.4.cloned.1.call-done.refs_2_, bf16[256,1024]{1,0:T(8,128)(2,1)S(1)} %constant_dynamic-slice_fusion, bf16[256,1024]{1,0:T(8,128)(2,1)S(1)} %copy-done.26), kind=kOutput, calls=%fused_computation.10 | convolution fusion | flops 1076363264 | bytes 4194304 | tf_op jit(solution)/shard_map/dot_general | solution.py:45
  122.0 1.1 fusion.17
  123.1 0.9 copy-done.35
  124.0 1.3 convolution_convert_fusion.2
  125.3 1.3 fusion.20
  126.6 1.1 fusion.16
  127.6 5.0 %collective-permute-start.17 = (bf16[256,1024]{1,0:T(8,128)(2,1)}, bf16[256,1024]{1,0:T(8,128)(2,1)S(1)}, u32[]{:S(2)}, u32[]{:S(2)}) collective-permute-start(bf16[256,1024]{1,0:T(8,128)(2,1)} %get-tuple-element.94), channel_id=1, source_target_pairs={{0,1},{1,0},{2,3},{3,2},{4,5},{5,4},{6,7},{7,6},{8,9},{9,8},{10,11... | collective-permute-start | bytes 1572872 | tf_op jit(solution)/shard_map/ppermute | solution.py:29
  132.7 2.6 %convolution_add_fusion.refs_4_ = f32[512,1024]{1,0:T(8,128)} fusion(f32[512,1024]{1,0:T(8,128)S(1)} %fusion.20, bf16[512,1024]{1,0:T(8,128)(2,1)S(1)} %copy-done.5, bf16[1024,1024]{1,0:T(8,128)(2,1)S(1)} %copy-done.15), kind=kOutput, calls=%fused_computation.8 | convolution fusion | flops 1074266112 | bytes 7340032 | tf_op jit(solution)/shard_map/dot_general | solution.py:45
  136.1 2.4 %line_own.1 = bf16[2048,512]{1,0:T(8,128)(2,1)} custom-call(bf16[512,512]{1,0:T(8,128)(2,1)} %get-tuple-element.87.refs_0_, bf16[512,512]{1,0:T(8,128)(2,1)} %copy-done.19, bf16[512,512]{1,0:T(8,128)(2,1)} %copy-done.20, bf16[512,512]{1,0:T(8,128)(2,1)} %copy-done.29, f32[512,1024]{1,0:T(8,128)} %convolution_add_fusion.refs_4_), custom_call_target="tpu_custom_call" | custom-call | flops 1 | bytes 1 | tf_op jit(solution)/shard_map/line_own/pallas_call | solution.py:115
  138.5 6.5 %fusion.21.refs_4_.refs_1_ = f32[512,1024]{1,0:T(8,128)} fusion(bf16[2048,512]{1,0:T(8,128)(2,1)} %line_own.1, bf16[2048,1024]{1,0:T(8,128)(2,1)} %all-gather.6.cloned.1.call-done), kind=kOutput, calls=%fused_computation.36 | convolution fusion | flops 2147483648 | bytes 8388608 | tf_op jit(solution)/shard_map/dot_general | solution.py:45
  145.1 1.0 copy-done.3
  146.0 1.8 last_part.1
  148.1 2.5 %collective-permute-start.21 = (f32[512,256]{1,0:T(8,128)}, f32[512,256]{1,0:T(8,128)}, u32[]{:S(2)}, u32[]{:S(2)}) collective-permute-start(f32[512,256]{1,0:T(8,128)} %get-tuple-element.89.refs_0_), channel_id=1, source_target_pairs={{0,48},{16,0},{32,16},{48,32},{64,112},{80,64},{96,80},{112,96},{1... | collective-permute-start | bytes 1572872 | tf_op jit(solution)/shard_map/ppermute | solution.py:335
  150.5 1.4 collective-permute-start.22
  151.9 2.7 %collective-permute-start.19 = (f32[256,1024]{1,0:T(8,128)}, f32[256,1024]{1,0:T(8,128)S(1)}, u32[]{:S(2)}, u32[]{:S(2)}) collective-permute-start(f32[256,1024]{1,0:T(8,128)} %get-tuple-element.88.refs_1_.refs_4_), channel_id=1, source_target_pairs={{0,2},{1,3},{2,0},{3,1},{4,6},{5,7},{6,4},{7,5},{8,10},{9,11},{10,... | collective-permute-start | bytes 3145736 | tf_op jit(solution)/shard_map/ppermute | solution.py:29
  155.5 2.6 %place_columns.2.refs_2_ = bf16[256,8192]{1,0:T(8,128)(2,1)} custom-call(bf16[256,1024]{1,0:T(8,128)(2,1)} %get-tuple-element.95.refs_5_.refs_0_, bf16[256,1024]{1,0:T(8,128)(2,1)} %copy-done.24, bf16[256,1024]{1,0:T(8,128)(2,1)} %get-tuple-element.93.refs_6_.refs_2_, bf16[256,1024]{1,0:T(8,128)(2,1)} %copy-done.25, ...), custom_call_target="tpu_custom_call" | custom-call | flops 1 | bytes 1 | tf_op jit(solution)/shard_map/place_columns/pallas_call | solution.py:115
  158.1 1.6 copy-done.12
  159.7 4.9 %slice_add_fusion.1.refs_5_ = f32[256,1024]{1,0:T(8,128)} fusion(f32[512,1024]{1,0:T(8,128)S(1)} %copy-done.12, bf16[2048,1024]{1,0:T(8,128)(2,1)} %a_line.1, bf16[512,2048]{1,0:T(8,128)(2,1)} %get-tuple-element.84), kind=kOutput, calls=%fused_computation.14 | convolution fusion | flops 1074003968 | bytes 7340032 | tf_op jit(solution)/shard_map/dot_general | solution.py:45
  164.6 2.3 %slice_add_fusion = f32[256,1024]{1,0:T(8,128)} fusion(f32[512,1024]{1,0:T(8,128)S(1)} %copy-done.12, bf16[2048,1024]{1,0:T(8,128)(2,1)S(1)} %copy-done.2, bf16[512,2048]{1,0:T(8,128)(2,1)S(1)} %copy-done.13), kind=kOutput, calls=%fused_computation.13 | convolution fusion | flops 1074003968 | bytes 7340032 | tf_op jit(solution)/shard_map/dot_general | solution.py:45
  166.9 1.9 collective-permute-start.15
  168.8 2.3 %convolution_convert_fusion = bf16[256,2048]{1,0:T(8,128)(2,1)} fusion(bf16[256,1024]{1,0:T(8,128)(2,1)S(1)} %copy-done.31, bf16[2048,1024]{1,0:T(8,128)(2,1)S(1)} %copy-done.2), kind=kOutput, calls=%fused_computation | convolution fusion | flops 1074266112 | bytes 5767168 | tf_op jit(solution)/shard_map/dot_general | solution.py:45
  171.1 2.3 %fusion.refs_0_.refs_4_ = bf16[256,2048]{1,0:T(8,128)(2,1)} fusion(bf16[2048,1024]{1,0:T(8,128)(2,1)S(1)} %copy-done.2, bf16[256,1024]{1,0:T(8,128)(2,1)S(1)} %copy-done.27), kind=kOutput, calls=%fused_computation.2 | convolution fusion | flops 1074266112 | bytes 5767168 | tf_op jit(solution)/shard_map/dot_general | solution.py:45
  173.4 2.4 %anchor_columns.1.refs_2_ = f32[512,1024]{1,0:T(8,128)} custom-call(f32[512,256]{1,0:T(8,128)} %get-tuple-element.89.refs_0_, f32[512,256]{1,0:T(8,128)} %collective-permute-done.20.refs_1_, f32[512,256]{1,0:T(8,128)} %collective-permute-done.21.refs_2_, f32[512,256]{1,0:T(8,128)} %collective-permute-done.22.refs_3_, bf16[256,2048]{1,0:T(8,128)(2,1)} %fusion.refs_0_.refs_4_, ...), custom_call_target="tpu_custom_call" | custom-call | flops 1 | bytes 1 | tf_op jit(solution)/shard_map/anchor_columns/pallas_call | solution.py:115
  175.9 1.0 copy-done.7
  176.9 0.9 copy-done
  177.8 2.7 %fusion.4 = bf16[1,512,1024]{2,1,0:T(8,128)(2,1)} fusion(f32[512,1024]{1,0:T(8,128)S(1)} %copy-done, bf16[1,4,512,1024]{3,2,1,0:T(8,128)(2,1)} %refs_3_.1, s32[]{:T(128)S(6)} %select_n.54), kind=kLoop, calls=%fused_computation.11 | loop fusion | flops 2097152 | bytes 4194308 | tf_op jit(solution)/shard_map/broadcast_in_dim | solution.py:366
  180.5 1.3 fusion.5
  181.8 2.2 %add_convert_fusion = bf16[256,1024]{1,0:T(8,128)(2,1)} fusion(f32[256,1024]{1,0:T(8,128)S(1)} %copy-done.9, f32[256,1024]{1,0:T(8,128)} %collective-permute-done.15), kind=kLoop, calls=%fused_computation.17 | loop fusion | flops 524288 | bytes 2621440 | tf_op jit(solution)/shard_map/convert_element_type | solution.py:359
  184.0 2.6 %place_columns.3 = bf16[256,8192]{1,0:T(8,128)(2,1)} custom-call(bf16[256,2048]{1,0:T(8,128)(2,1)} %fusion.refs_0_.refs_4_, bf16[256,2048]{1,0:T(8,128)(2,1)} %collective-permute-done.16.refs_1_, bf16[256,8192]{1,0:T(8,128)(2,1)} %place_columns.2.refs_2_), custom_call_target="tpu_custom_call", output_to_operand_aliasing={{}: (2, {})} | custom-call | flops 1 | bytes 1 | tf_op jit(solution)/shard_map/place_columns/pallas_call | solution.py:115
  (101 shorter events, 3.6 us)
Async XLA Ops:
  7.2 48.4 %all-gather.4.cloned.1.call-start = ((), (), s32[]{:S(2)}) async-start(), calls=%async_computation | async-start | bytes 2621440 | tf_op jit(solution)/shard_map/all_gather | solution.py:41
  10.0 7.8 %copy-start.28 = (bf16[256,1024]{1,0:T(8,128)(2,1)S(1)}, bf16[256,1024]{1,0:T(8,128)(2,1)}, u32[]{:S(2)}) copy-start(bf16[256,1024]{1,0:T(8,128)(2,1)} %get-tuple-element.48.refs_0_) | copy-start | bytes 1572868
  10.0 88.5 %all-gather.6.cloned.1.call-start = ((), (), s32[]{:S(2)}) async-start(), calls=%async_computation.1 | async-start | bytes 4718592 | tf_op jit(solution)/shard_map/all_gather | solution.py:41
  16.2 141.9 %all-gather.8.cloned.1.call-start = ((), (), s32[]{:S(2)}) async-start(), calls=%async_computation.2 | async-start | bytes 5242880 | tf_op jit(solution)/shard_map/all_gather | solution.py:41
  16.3 5.5 %collective-permute-start.2 = (bf16[8,256,512]{2,1,0:T(8,128)(2,1)}, bf16[8,256,512]{2,1,0:T(8,128)(2,1)S(1)}, u32[]{:S(2)}, u32[]{:S(2)}) collective-permute-start(bf16[8,256,512]{2,1,0:T(8,128)(2,1)} %get-tuple-element.51), channel_id=1, source_target_pairs={{0,1},{1,0},{2,3},{3,2},{4,5},{5,4},{6,7},{7,6},{8,9},{9,8},{10,11... | collective-permute-start | bytes 6291464 | tf_op jit(solution)/shard_map/ppermute | solution.py:29
  17.8 15.1 %collective-permute-start = (bf16[256,1024]{1,0:T(8,128)(2,1)S(1)}, bf16[256,1024]{1,0:T(8,128)(2,1)}, u32[]{:S(2)}, u32[]{:S(2)}) collective-permute-start(bf16[256,1024]{1,0:T(8,128)(2,1)S(1)} %copy-done.28), channel_id=1, source_target_pairs={{0,2},{1,3},{2,0},{3,1},{4,6},{5,7},{6,4},{7,5},{8,10},{9,11},{10,... | collective-permute-start | bytes 1572872 | tf_op jit(solution)/shard_map/ppermute | solution.py:29
  20.6 23.7 %collective-permute-start.1 = (bf16[512,512]{1,0:T(8,128)(2,1)}, bf16[512,512]{1,0:T(8,128)(2,1)S(1)}, u32[]{:S(2)}, u32[]{:S(2)}) collective-permute-start(bf16[512,512]{1,0:T(8,128)(2,1)} %get-tuple-element.50), channel_id=1, source_target_pairs={{0,64},{16,80},{32,96},{48,112},{64,0},{80,16},{96,32},{112,48},{1... | collective-permute-start | bytes 1572872 | tf_op jit(solution)/shard_map/ppermute | solution.py:37
  21.8 1.3 copy-start.14
  26.3 26.7 %collective-permute-start.3 = (bf16[512,512]{1,0:T(8,128)(2,1)}, bf16[512,512]{1,0:T(8,128)(2,1)S(1)}, u32[]{:S(2)}, u32[]{:S(2)}) collective-permute-start(bf16[512,512]{1,0:T(8,128)(2,1)} %get-tuple-element.63), channel_id=1, source_target_pairs={{0,4},{1,5},{2,6},{3,7},{4,8},{5,9},{6,10},{7,11},{8,12},{9,13},{1... | collective-permute-start | bytes 1572872 | tf_op jit(solution)/shard_map/ppermute | solution.py:29
  27.8 33.5 %copy-start.34 = (s32[4]{0:T(128)S(1)}, s32[4]{0:T(128)}, u32[]{:S(2)}) copy-start(s32[4]{0:T(128)} %refs_0_.3) | copy-start | bytes 52
  27.8 25.2 %collective-permute-start.4 = (bf16[512,512]{1,0:T(8,128)(2,1)}, bf16[512,512]{1,0:T(8,128)(2,1)S(1)}, u32[]{:S(2)}, u32[]{:S(2)}) collective-permute-start(bf16[512,512]{1,0:T(8,128)(2,1)} %get-tuple-element.64), channel_id=1, source_target_pairs={{0,12},{1,13},{2,14},{3,15},{4,0},{5,1},{6,2},{7,3},{8,4},{9,5},{1... | collective-permute-start | bytes 1572872 | tf_op jit(solution)/shard_map/ppermute | solution.py:29
  44.3 11.3 %copy-start.16 = (bf16[512,512]{1,0:T(8,128)(2,1)}, bf16[512,512]{1,0:T(8,128)(2,1)S(1)}, u32[]{:S(2)}) copy-start(bf16[512,512]{1,0:T(8,128)(2,1)S(1)} %collective-permute-done.1.refs_3_) | copy-start | bytes 1572868
  53.0 2.6 %copy-start.17 = (bf16[512,512]{1,0:T(8,128)(2,1)}, bf16[512,512]{1,0:T(8,128)(2,1)S(1)}, u32[]{:S(2)}) copy-start(bf16[512,512]{1,0:T(8,128)(2,1)S(1)} %collective-permute-done.3.refs_4_.refs_1_) | copy-start | bytes 1572868
  53.0 2.6 %copy-start.18 = (bf16[512,512]{1,0:T(8,128)(2,1)}, bf16[512,512]{1,0:T(8,128)(2,1)S(1)}, u32[]{:S(2)}) copy-start(bf16[512,512]{1,0:T(8,128)(2,1)S(1)} %collective-permute-done.4.refs_5_.refs_2_) | copy-start | bytes 1572868
  58.5 25.9 %collective-permute-start.5 = (bf16[512,1024]{1,0:T(8,128)(2,1)}, bf16[512,1024]{1,0:T(8,128)(2,1)S(1)}, u32[]{:S(2)}, u32[]{:S(2)}) collective-permute-start(bf16[512,1024]{1,0:T(8,128)(2,1)} %get-tuple-element.65), channel_id=1, source_target_pairs={{0,2},{1,3},{2,0},{3,1},{4,6},{5,7},{6,4},{7,5},{8,10},{9,11},{10,... | collective-permute-start | bytes 3145736 | tf_op jit(solution)/shard_map/ppermute | solution.py:29
  61.4 18.4 %collective-permute-start.6 = (bf16[512,512]{1,0:T(8,128)(2,1)}, bf16[512,512]{1,0:T(8,128)(2,1)}, u32[]{:S(2)}, u32[]{:S(2)}) collective-permute-start(bf16[512,512]{1,0:T(8,128)(2,1)} %get-tuple-element.67), channel_id=1, source_target_pairs={{0,8},{1,9},{2,10},{3,11},{4,12},{5,13},{6,14},{7,15},{8,0},{9,1},... | collective-permute-start | bytes 1572872 | tf_op jit(solution)/shard_map/ppermute | solution.py:29
  64.6 15.3 %collective-permute-start.7 = (f32[512,256]{1,0:T(8,128)S(1)}, f32[512,256]{1,0:T(8,128)S(1)}, u32[]{:S(2)}, u32[]{:S(2)}) collective-permute-start(f32[512,256]{1,0:T(8,128)S(1)} %constant_dynamic-slice_fusion.2), channel_id=1, source_target_pairs={{0,32},{16,48},{32,0},{48,16},{64,96},{80,112},{96,64},{112,80},{1... | collective-permute-start | bytes 1572872 | tf_op jit(solution)/shard_map/ppermute | solution.py:37
  79.9 4.5 %copy-start.22 = (f32[512,256]{1,0:T(8,128)}, f32[512,256]{1,0:T(8,128)S(1)}, u32[]{:S(2)}) copy-start(f32[512,256]{1,0:T(8,128)S(1)} %collective-permute-done.7.refs_6_) | copy-start | bytes 1572868
  84.4 1.0 copy-start.10
  87.9 5.3 %copy-start.21 = (bf16[512,512]{1,0:T(8,128)(2,1)S(1)}, bf16[512,512]{1,0:T(8,128)(2,1)}, u32[]{:S(2)}) copy-start(bf16[512,512]{1,0:T(8,128)(2,1)} %get-tuple-element.79) | copy-start | bytes 1572868
  87.9 8.0 %copy-start.32 = (f32[512,128]{1,0:T(8,128)S(1)}, f32[512,128]{1,0:T(8,128)}, u32[]{:S(2)}) copy-start(f32[512,128]{1,0:T(8,128)} %param.11) | copy-start | bytes 786436
  89.1 6.7 %collective-permute-start.11 = (f32[512,128]{1,0:T(8,128)S(1)}, f32[512,128]{1,0:T(8,128)S(1)}, u32[]{:S(2)}, u32[]{:S(2)}) collective-permute-start(f32[512,128]{1,0:T(8,128)S(1)} %constant_dynamic-slice_fusion.1), channel_id=1, source_target_pairs={{0,16},{16,0},{32,48},{48,32},{64,80},{80,64},{96,112},{112,96},{1... | collective-permute-start | bytes 786440 | tf_op jit(solution)/shard_map/ppermute | solution.py:37
  90.5 24.7 %collective-permute-start.8 = (bf16[512,1024]{1,0:T(8,128)(2,1)}, bf16[512,1024]{1,0:T(8,128)(2,1)}, u32[]{:S(2)}, u32[]{:S(2)}) collective-permute-start(bf16[512,1024]{1,0:T(8,128)(2,1)} %get-tuple-element.72), channel_id=1, source_target_pairs={{0,2},{1,3},{2,0},{3,1},{4,6},{5,7},{6,4},{7,5},{8,10},{9,11},{10,... | collective-permute-start | bytes 3145736 | tf_op jit(solution)/shard_map/ppermute | solution.py:29
  93.2 13.7 %collective-permute-start.9 = (bf16[512,512]{1,0:T(8,128)(2,1)S(1)}, bf16[512,512]{1,0:T(8,128)(2,1)S(1)}, u32[]{:S(2)}, u32[]{:S(2)}) collective-permute-start(bf16[512,512]{1,0:T(8,128)(2,1)S(1)} %copy-done.21), channel_id=1, source_target_pairs={{0,4},{1,5},{2,6},{3,7},{4,8},{5,9},{6,10},{7,11},{8,12},{9,13},{1... | collective-permute-start | bytes 1572872 | tf_op jit(solution)/shard_map/ppermute | solution.py:29
  93.2 13.7 %collective-permute-start.10 = (bf16[512,512]{1,0:T(8,128)(2,1)}, bf16[512,512]{1,0:T(8,128)(2,1)S(1)}, u32[]{:S(2)}, u32[]{:S(2)}) collective-permute-start(bf16[512,512]{1,0:T(8,128)(2,1)} %get-tuple-element.80), channel_id=1, source_target_pairs={{0,12},{1,13},{2,14},{3,15},{4,0},{5,1},{6,2},{7,3},{8,4},{9,5},{1... | collective-permute-start | bytes 1572872 | tf_op jit(solution)/shard_map/ppermute | solution.py:29
  97.6 4.8 %copy-start.23 = (f32[512,128]{1,0:T(8,128)}, f32[512,128]{1,0:T(8,128)S(1)}, u32[]{:S(2)}) copy-start(f32[512,128]{1,0:T(8,128)S(1)} %get-tuple-element.90.refs_0_) | copy-start | bytes 786436
  97.6 47.4 %collective-permute-start.12 = (f32[512,128]{1,0:T(8,128)S(1)}, f32[512,128]{1,0:T(8,128)}, u32[]{:S(2)}, u32[]{:S(2)}) collective-permute-start(f32[512,128]{1,0:T(8,128)S(1)} %get-tuple-element.90.refs_0_), channel_id=1, source_target_pairs={{0,64},{16,80},{32,96},{48,112},{64,0},{80,16},{96,32},{112,48},{1... | collective-permute-start | bytes 786440 | tf_op jit(solution)/shard_map/ppermute | solution.py:37
  98.5 6.2 %copy-start.33 = (bf16[2048,1024]{1,0:T(8,128)(2,1)S(1)}, bf16[2048,1024]{1,0:T(8,128)(2,1)}, u32[]{:S(2)}) copy-start(bf16[2048,1024]{1,0:T(8,128)(2,1)} %all-gather.6.cloned.1.call-done) | copy-start | bytes 12582916
  98.5 6.2 %copy-start.36 = (bf16[2048,256]{1,0:T(8,128)(2,1)S(1)}, bf16[2048,256]{1,0:T(8,128)(2,1)}, u32[]{:S(2)}) copy-start(bf16[2048,256]{1,0:T(8,128)(2,1)} %get-tuple-element.77) | copy-start | bytes 3145732
  102.4 4.5 %copy-start.11 = (f32[256,1024]{1,0:T(8,128)}, f32[256,1024]{1,0:T(8,128)S(1)}, u32[]{:S(2)}) copy-start(f32[256,1024]{1,0:T(8,128)S(1)} %fusion.18.refs_3_.refs_4_) | copy-start | bytes 3145732
  102.4 42.6 %collective-permute-start.13 = (f32[256,1024]{1,0:T(8,128)S(1)}, f32[256,1024]{1,0:T(8,128)S(1)}, u32[]{:S(2)}, u32[]{:S(2)}) collective-permute-start(f32[256,1024]{1,0:T(8,128)S(1)} %fusion.18.refs_3_.refs_4_), channel_id=1, source_target_pairs={{0,2},{1,3},{2,0},{3,1},{4,6},{5,7},{6,4},{7,5},{8,10},{9,11},{10,... | collective-permute-start | bytes 3145736 | tf_op jit(solution)/shard_map/ppermute | solution.py:29
  106.9 0.8 copy-start.19
  106.9 1.0 copy-start.20
  107.9 27.4 %collective-permute-start.14 = (bf16[512,512]{1,0:T(8,128)(2,1)}, bf16[512,512]{1,0:T(8,128)(2,1)S(1)}, u32[]{:S(2)}, u32[]{:S(2)}) collective-permute-start(bf16[512,512]{1,0:T(8,128)(2,1)} %last_cols.1.refs_6_), channel_id=1, source_target_pairs={{0,8},{1,9},{2,10},{3,11},{4,12},{5,13},{6,14},{7,15},{8,0},{9,1},... | collective-permute-start | bytes 1572872 | tf_op jit(solution)/shard_map/ppermute | solution.py:29
  115.2 3.7 %copy-start.26 = (bf16[256,1024]{1,0:T(8,128)(2,1)S(1)}, bf16[256,1024]{1,0:T(8,128)(2,1)}, u32[]{:S(2)}) copy-start(bf16[256,1024]{1,0:T(8,128)(2,1)} %refs_2_.1) | copy-start | bytes 1572868
  118.9 4.1 %copy-start.30 = (bf16[256,1024]{1,0:T(8,128)(2,1)}, bf16[256,1024]{1,0:T(8,128)(2,1)S(1)}, u32[]{:S(2)}) copy-start(bf16[256,1024]{1,0:T(8,128)(2,1)S(1)} %constant_dynamic-slice_fusion) | copy-start | bytes 1572868
  122.0 2.0 %copy-start.35 = (bf16[1024,1024]{1,0:T(8,128)(2,1)S(1)}, bf16[1024,1024]{1,0:T(8,128)(2,1)}, u32[]{:S(2)}) copy-start(bf16[1024,1024]{1,0:T(8,128)(2,1)} %get-tuple-element.83) | copy-start | bytes 6291460
  124.0 1.3 copy-start.6
  125.3 7.4 %copy-start.15 = (bf16[1024,1024]{1,0:T(8,128)(2,1)S(1)}, bf16[1024,1024]{1,0:T(8,128)(2,1)}, u32[]{:S(2)}) copy-start(bf16[1024,1024]{1,0:T(8,128)(2,1)} %all-gather.4.cloned.1.call-done.refs_2_) | copy-start | bytes 6291460
  126.6 6.1 %copy-start.5 = (bf16[512,1024]{1,0:T(8,128)(2,1)S(1)}, bf16[512,1024]{1,0:T(8,128)(2,1)}, u32[]{:S(2)}) copy-start(bf16[512,1024]{1,0:T(8,128)(2,1)} %get-tuple-element.81) | copy-start | bytes 3145732
  127.6 24.3 %collective-permute-start.17 = (bf16[256,1024]{1,0:T(8,128)(2,1)}, bf16[256,1024]{1,0:T(8,128)(2,1)S(1)}, u32[]{:S(2)}, u32[]{:S(2)}) collective-permute-start(bf16[256,1024]{1,0:T(8,128)(2,1)} %get-tuple-element.94), channel_id=1, source_target_pairs={{0,1},{1,0},{2,3},{3,2},{4,5},{5,4},{6,7},{7,6},{8,9},{9,8},{10,11... | collective-permute-start | bytes 1572872 | tf_op jit(solution)/shard_map/ppermute | solution.py:29
  132.7 22.0 %collective-permute-start.18 = (bf16[256,1024]{1,0:T(8,128)(2,1)}, bf16[256,1024]{1,0:T(8,128)(2,1)S(1)}, u32[]{:S(2)}, u32[]{:S(2)}) collective-permute-start(bf16[256,1024]{1,0:T(8,128)(2,1)} %get-tuple-element.92), channel_id=1, source_target_pairs={{0,1},{1,0},{2,3},{3,2},{4,5},{5,4},{6,7},{7,6},{8,9},{9,8},{10,11... | collective-permute-start | bytes 1572872 | tf_op jit(solution)/shard_map/ppermute | solution.py:29
  135.3 0.8 copy-start.29
  145.0 1.0 copy-start.3
  147.8 23.3 %collective-permute-start.20 = (f32[512,256]{1,0:T(8,128)}, f32[512,256]{1,0:T(8,128)}, u32[]{:S(2)}, u32[]{:S(2)}) collective-permute-start(f32[512,256]{1,0:T(8,128)} %get-tuple-element.89.refs_0_), channel_id=1, source_target_pairs={{0,16},{16,32},{32,48},{48,0},{64,80},{80,96},{96,112},{112,64},{1... | collective-permute-start | bytes 1572872 | tf_op jit(solution)/shard_map/ppermute | solution.py:335
  148.1 25.3 %collective-permute-start.21 = (f32[512,256]{1,0:T(8,128)}, f32[512,256]{1,0:T(8,128)}, u32[]{:S(2)}, u32[]{:S(2)}) collective-permute-start(f32[512,256]{1,0:T(8,128)} %get-tuple-element.89.refs_0_), channel_id=1, source_target_pairs={{0,48},{16,0},{32,16},{48,32},{64,112},{80,64},{96,80},{112,96},{1... | collective-permute-start | bytes 1572872 | tf_op jit(solution)/shard_map/ppermute | solution.py:335
  150.5 22.9 %collective-permute-start.22 = (f32[512,256]{1,0:T(8,128)}, f32[512,256]{1,0:T(8,128)}, u32[]{:S(2)}, u32[]{:S(2)}) collective-permute-start(f32[512,256]{1,0:T(8,128)} %get-tuple-element.89.refs_0_), channel_id=1, source_target_pairs={{0,32},{16,48},{32,0},{48,16},{64,96},{80,112},{96,64},{112,80},{1... | collective-permute-start | bytes 1572872 | tf_op jit(solution)/shard_map/ppermute | solution.py:335
  151.9 2.8 %copy-start.24 = (bf16[256,1024]{1,0:T(8,128)(2,1)}, bf16[256,1024]{1,0:T(8,128)(2,1)S(1)}, u32[]{:S(2)}) copy-start(bf16[256,1024]{1,0:T(8,128)(2,1)S(1)} %collective-permute-done.17.refs_1_) | copy-start | bytes 1572868
  151.9 23.9 %collective-permute-start.19 = (f32[256,1024]{1,0:T(8,128)}, f32[256,1024]{1,0:T(8,128)S(1)}, u32[]{:S(2)}, u32[]{:S(2)}) collective-permute-start(f32[256,1024]{1,0:T(8,128)} %get-tuple-element.88.refs_1_.refs_4_), channel_id=1, source_target_pairs={{0,2},{1,3},{2,0},{3,1},{4,6},{5,7},{6,4},{7,5},{8,10},{9,11},{10,... | collective-permute-start | bytes 3145736 | tf_op jit(solution)/shard_map/ppermute | solution.py:29
  154.7 0.8 copy-start.25
  158.1 1.6 copy-start.12
  159.7 4.9 %copy-start.2 = (bf16[2048,1024]{1,0:T(8,128)(2,1)S(1)}, bf16[2048,1024]{1,0:T(8,128)(2,1)}, u32[]{:S(2)}) copy-start(bf16[2048,1024]{1,0:T(8,128)(2,1)} %a_line.1) | copy-start | bytes 12582916
  159.7 4.9 %copy-start.13 = (bf16[512,2048]{1,0:T(8,128)(2,1)S(1)}, bf16[512,2048]{1,0:T(8,128)(2,1)}, u32[]{:S(2)}) copy-start(bf16[512,2048]{1,0:T(8,128)(2,1)} %get-tuple-element.84) | copy-start | bytes 6291460
  164.6 4.2 %copy-start.31 = (bf16[256,1024]{1,0:T(8,128)(2,1)S(1)}, bf16[256,1024]{1,0:T(8,128)(2,1)}, u32[]{:S(2)}) copy-start(bf16[256,1024]{1,0:T(8,128)(2,1)} %copy-done.30) | copy-start | bytes 1572868
  166.9 4.2 %copy-start.27 = (bf16[256,1024]{1,0:T(8,128)(2,1)S(1)}, bf16[256,1024]{1,0:T(8,128)(2,1)}, u32[]{:S(2)}) copy-start(bf16[256,1024]{1,0:T(8,128)(2,1)} %refs_2_.1) | copy-start | bytes 1572868
  166.9 14.9 %collective-permute-start.15 = (f32[256,1024]{1,0:T(8,128)}, f32[256,1024]{1,0:T(8,128)}, u32[]{:S(2)}, u32[]{:S(2)}) collective-permute-start(f32[256,1024]{1,0:T(8,128)} %slice_add_fusion), channel_id=1, source_target_pairs={{0,1},{1,0},{2,3},{3,2},{4,5},{5,4},{6,7},{7,6},{8,9},{9,8},{10,11... | collective-permute-start | bytes 3145736 | tf_op jit(solution)/shard_map/ppermute | solution.py:29
  171.1 12.9 %collective-permute-start.16 = (bf16[256,2048]{1,0:T(8,128)(2,1)}, bf16[256,2048]{1,0:T(8,128)(2,1)}, u32[]{:S(2)}, u32[]{:S(2)}) collective-permute-start(bf16[256,2048]{1,0:T(8,128)(2,1)} %convolution_convert_fusion), channel_id=1, source_target_pairs={{0,1},{1,0},{2,3},{3,2},{4,5},{5,4},{6,7},{7,6},{8,9},{9,8},{10,11... | collective-permute-start | bytes 3145736 | tf_op jit(solution)/shard_map/ppermute | solution.py:29
  175.8 2.0 %copy-start = (f32[512,1024]{1,0:T(8,128)S(1)}, f32[512,1024]{1,0:T(8,128)}, u32[]{:S(2)}) copy-start(f32[512,1024]{1,0:T(8,128)} %anchor_columns.1.refs_2_) | copy-start | bytes 6291460
  175.9 1.0 copy-start.7
  177.8 2.7 %copy-start.1 = (f32[512,1024]{1,0:T(8,128)S(1)}, f32[512,1024]{1,0:T(8,128)}, u32[]{:S(2)}) copy-start(f32[512,1024]{1,0:T(8,128)} %fusion.21.refs_4_.refs_1_) | copy-start | bytes 6291460
  177.8 2.7 %copy-start.4 = (f32[256,1024]{1,0:T(8,128)S(1)}, f32[256,1024]{1,0:T(8,128)}, u32[]{:S(2)}) copy-start(f32[256,1024]{1,0:T(8,128)} %copy-done.3) | copy-start | bytes 3145732
  177.8 2.7 %copy-start.8 = (f32[256,1024]{1,0:T(8,128)S(1)}, f32[256,1024]{1,0:T(8,128)}, u32[]{:S(2)}) copy-start(f32[256,1024]{1,0:T(8,128)} %rest.1) | copy-start | bytes 3145732
  180.5 1.3 copy-start.9
Sparse Core Ops, SparseCore 0:
  10.2 45.2 all-gather.3
  57.2 38.5 all-gather.5
  97.5 57.3 all-gather.7
